TPU v7x, 512 devices: a whole 4x4x16 slice. The times are simulated.
512 devices in a mesh: dp: 8 (over x, core), expert: 64 (over z, y).
Axes of the slice: x: 4, y: 4, z: 16, core: 2. Of those that a mesh axis runs over, the one named last changes fastest.
Arguments:
- x_stash: bfloat16 [8192, 1440], P('expert', 'dp'), may hold values from -6 to 6
- out_grad: bfloat16 [8192, 1440], P('expert', 'dp'), may hold values from -6 to 6
- expert_ids: int32 [4, 8192], replicated, may hold values from 0 to 63, as said below
- gates: float32 [4, 8192], replicated, may hold values from 0.1 to 1
- scales: float32 [8192], replicated, may hold values from 0.25 to 4
- w_gate: bfloat16 [64, 1440, 2048], P('expert', None, 'dp'), may hold values from -0.15625 to 0.15625
- w_up: bfloat16 [64, 1440, 2048], P('expert', None, 'dp'), may hold values from -0.15625 to 0.15625
- w_down: bfloat16 [64, 2048, 1440], P('expert', 'dp'), may hold values from -0.125 to 0.125
Outputs:
- grad_input: bfloat16 [8192, 1440], P('expert', 'dp')
- grad_gate: bfloat16 [64, 1440, 2048], P('expert', None, 'dp')
- grad_up: bfloat16 [64, 1440, 2048], P('expert', None, 'dp')
- grad_down: bfloat16 [64, 2048, 1440], P('expert', 'dp')
Inputs may be any that keep to these rules, and one draw needn't show every extreme that they name: `expert_ids`: each token names 4 different experts. In each aligned block of 128 tokens, no expert is named by more than 16 tokens, and some expert is named by exactly 16 tokens of some block.
All inputs are finite; a program needn't handle non-finite values.
Results may differ from a plain program's by a relative error of at most 0.02.
Values may be sent and summed in bfloat16 or wider, within the bound.
A program may use at most 64 MiB of HBM per device.

v0:
```python
import jax
import jax.numpy as jnp
from jax import lax
from jax.sharding import PartitionSpec as P

TOP = 4


def slot_onehot(hit, slots_per):
    rank = jnp.cumsum(hit, axis=-1, dtype=jnp.int32) - hit
    slot_iota = lax.broadcasted_iota(jnp.int32, (1, slots_per, 1), 1)
    return (rank[:, None, :] == slot_iota) & (hit[:, None, :] == 1)


def expert_math(xs, dys, gate, weight_gate, weight_up, weight_down):
    g = jnp.dot(xs, weight_gate, preferred_element_type=jnp.float32)
    u = jnp.dot(xs, weight_up, preferred_element_type=jnp.float32)
    sig = jax.nn.sigmoid(g)
    act = (gate[:, None] * (g * sig * u)).astype(jnp.bfloat16)
    dsum = lax.dot_general(
        dys, weight_down, (((1,), (1,)), ((), ())), preferred_element_type=jnp.float32
    )
    d_a = gate[:, None] * dsum
    d_gate = (d_a * u * sig * (1.0 + g * (1.0 - sig))).astype(jnp.bfloat16)
    d_up = (d_a * g * sig).astype(jnp.bfloat16)
    first = (((0,), (0,)), ((), ()))
    grad_down = lax.dot_general(act, dys, first, preferred_element_type=jnp.float32)
    grad_gate = lax.dot_general(xs, d_gate, first, preferred_element_type=jnp.float32)
    grad_up = lax.dot_general(xs, d_up, first, preferred_element_type=jnp.float32)
    second = (((1,), (1,)), ((), ()))
    partial_value = lax.dot_general(d_gate, weight_gate, second, preferred_element_type=jnp.float32)
    partial_value = partial_value + lax.dot_general(
        d_up, weight_up, second, preferred_element_type=jnp.float32
    )
    return (grad_gate, grad_up, grad_down, partial_value.astype(jnp.bfloat16))


def on_device(x_stash, out_grad, expert_ids, gates, scales, w_gate, w_up, w_down):
    tok_dev, slice_width = x_stash.shape
    width = w_gate.shape[1]
    groups = lax.axis_size("expert")
    slots_per = 2 * tok_dev * TOP // groups
    owner = lax.axis_index("expert")
    named = expert_ids == owner
    weight = jnp.sum(jnp.where(named, gates, jnp.float32(0.0)), axis=0).reshape(groups, tok_dev)
    hit = jnp.any(named, axis=0).astype(jnp.int32).reshape(groups, tok_dev)
    mine = slot_onehot(hit, slots_per)
    mine_float = mine.astype(jnp.float32)
    slot_gate = jnp.sum(mine_float * weight[:, None, :], axis=2).reshape(-1)
    slot_scale = jnp.sum(mine_float * scales.reshape(groups, tok_dev)[:, None, :], axis=2).reshape(
        -1
    )
    own_ids = lax.dynamic_slice_in_dim(expert_ids, owner * tok_dev, tok_dev, 1)
    expert_iota = lax.broadcasted_iota(jnp.int32, (groups, 1, 1), 0)
    member = jnp.any(own_ids[None, :, :] == expert_iota, axis=1).astype(jnp.int32)
    sent = slot_onehot(member, slots_per)
    every_x, every_dy = (
        lax.all_gather(x_stash, "expert", axis=0, tiled=True),
        lax.all_gather(out_grad, "expert", axis=0, tiled=True),
    )
    starts = lax.broadcasted_iota(jnp.int32, (groups, 1, 1), 0) * tok_dev
    position = lax.broadcasted_iota(jnp.int32, (1, 1, tok_dev), 2)
    rows = jnp.sum(mine.astype(jnp.int32) * (starts + position), axis=2, dtype=jnp.int32).reshape(
        -1
    )
    picked_x = jnp.take(every_x, rows, axis=0)
    picked_dy = jnp.take(every_dy, rows, axis=0)
    xs, dys = (
        lax.all_gather(picked_x, "dp", axis=1, tiled=True),
        lax.all_gather(picked_dy, "dp", axis=1, tiled=True),
    )
    xs = (xs.astype(jnp.float32) * slot_scale[:, None]).astype(jnp.bfloat16)
    grad_gate, grad_up, grad_down, partial_value = expert_math(
        xs, dys, slot_gate, w_gate[0], w_up[0], w_down[0]
    )
    partial_value = partial_value.reshape(groups, slots_per, width)
    spread = lax.optimization_barrier(partial_value).astype(jnp.float32)
    summed = lax.psum_scatter(
        spread.astype(jnp.bfloat16), "dp", scatter_dimension=2, tiled=True
    ).astype(jnp.float32)
    back = lax.all_to_all(
        summed.astype(jnp.bfloat16), "expert", split_axis=0, concat_axis=0, tiled=True
    ).astype(summed.dtype)
    grad_input = jnp.einsum(
        "ect,ecf->tf", sent.astype(jnp.float32), back, precision=lax.Precision.HIGHEST
    )
    return (
        grad_input.astype(jnp.bfloat16),
        grad_gate[None].astype(jnp.bfloat16),
        grad_up[None].astype(jnp.bfloat16),
        grad_down[None].astype(jnp.bfloat16),
    )


def solution(mesh):
    return jax.shard_map(
        on_device,
        mesh=mesh,
        in_specs=(
            P("expert", "dp"),
            P("expert", "dp"),
            P(),
            P(),
            P(),
            P("expert", None, "dp"),
            P("expert", None, "dp"),
            P("expert", "dp", None),
        ),
        out_specs=(
            P("expert", "dp"),
            P("expert", None, "dp"),
            P("expert", None, "dp"),
            P("expert", "dp", None),
        ),
        check_vma=False,
    )
```

profile of v0, /device:TPU:1, one launch (start us, length us, event | category | flops | bytes accessed | tf_op | source)
XLA Modules:
  0.0 541.3 jit_solution(8551746856430230633)
XLA Ops:
  7.2 1.6 copy.31
  8.8 0.0 all-gather.7.cloned.1.call-start
  8.9 1.5 copy.29
  10.4 0.0 all-gather.13.cloned.1.call-start
  10.5 1.1 select_reduce_fusion.3
  11.6 0.1 reduce_or.19
  11.7 0.3 reduce_window_sum.18
  12.0 0.1 iota_add_fusion
  12.1 1.2 select_reduce_fusion.1
  13.2 0.1 reshape.97
  13.3 142.0 %all-gather.9.cloned.1.call-done = bf16[8192,180]{1,0:T(8,128)(2,1)} async-done(((bf16[128,180]{1,0:T(8,128)(2,1)}), bf16[8192,180]{1,0:T(8,128)(2,1)}) %all-gather.9.cloned.1.call-update) | async-done | bytes 2949136 | tf_op jit(solution)/shard_map/all_gather | solution.py:58
  155.4 6.2 %gather_fusion.1 = bf16[1024,180]{1,0:T(8,128)(2,1)S(1)} fusion(bf16[8192,180]{1,0:T(8,128)(2,1)} %all-gather.9.cloned.1.call-done, s32[1024]{0:T(1024)S(1)} %fusion.23), kind=kCustom, calls=%fused_computation.1.clone | custom fusion | bytes 741376 | tf_op jit(solution)/shard_map/jit(_take)/gather | solution.py:66
  161.6 138.6 %all-gather.7.cloned.1.call-done = bf16[8192,180]{1,0:T(8,128)(2,1)} async-done(((bf16[128,180]{1,0:T(8,128)(2,1)}), bf16[8192,180]{1,0:T(8,128)(2,1)}) %all-gather.7.cloned.1.call-update) | async-done | bytes 2949136 | tf_op jit(solution)/shard_map/all_gather | solution.py:59
  300.1 6.2 %gather_fusion = bf16[1024,180]{1,0:T(8,128)(2,1)S(1)} fusion(bf16[8192,180]{1,0:T(8,128)(2,1)} %all-gather.7.cloned.1.call-done, s32[1024]{0:T(1024)S(1)} %fusion.23), kind=kCustom, calls=%fused_computation.clone | custom fusion | bytes 741376 | tf_op jit(solution)/shard_map/jit(_take)/gather | solution.py:67
  306.3 0.2 select_bitcast_fusion.1
  306.5 0.9 copy.32
  307.5 0.0 all-gather.11.cloned.1.call-start
  307.5 0.9 copy.30
  308.5 0.2 all-reduce.3.cloned.1.call-start
  308.7 0.4 select_reduce_fusion.2
  309.1 0.1 mul.96
  309.2 0.1 mul.106
  309.2 36.4 %all-gather.13.cloned.1.call-done = bf16[8,180,1024]{2,1,0:T(8,128)(2,1)} async-done(((bf16[1,180,1024]{2,1,0:T(8,128)(2,1)}), bf16[8,180,1024]{2,1,0:T(8,128)(2,1)}) %all-gather.13.cloned.1.call-update) | async-done | bytes 2949136 | tf_op jit(solution)/shard_map/all_gather | solution.py:69
  345.6 5.0 reshape.122
  350.6 3.5 multiply_convert_fusion
  354.2 2.0 fusion.6
  356.2 2.0 fusion.9
  358.2 25.1 %all-gather.11.cloned.1.call-done = bf16[8,180,1024]{2,1,0:T(8,128)(2,1)} async-done(((bf16[1,180,1024]{2,1,0:T(8,128)(2,1)}), bf16[8,180,1024]{2,1,0:T(8,128)(2,1)}) %all-gather.11.cloned.1.call-update) | async-done | bytes 2949136 | tf_op jit(solution)/shard_map/all_gather | solution.py:70
  383.4 4.3 reshape.119
  387.7 3.8 multiply_convert_fusion.2
  391.5 1.0 fusion.4
  392.5 2.6 add_convert_fusion
  395.1 4.6 copy.33
  399.7 5.3 copy.34
  405.0 1.3 dynamic-slice
  406.9 0.7 constant_dynamic-slice_fusion.1
  407.6 80.0 %all-reduce.3.cloned.1.call-done = bf16[64,16,1440]{2,0,1:T(8,128)(2,1)} async-done(((bf16[64,16,1440]{2,0,1:T(8,128)(2,1)}), bf16[64,16,1440]{2,0,1:T(8,128)(2,1)}) %all-reduce.3.cloned.1.call-update) | async-done | bytes 2949136
  487.6 1.4 constant_dynamic-slice_fusion
  489.0 1.1 copy.35
  490.1 15.6 %all-to-all-start = ((bf16[64,16,180]{2,1,0:T(8,128)(2,1)}), bf16[64,16,180]{2,1,0:T(8,128)(2,1)S(1)}, u32[]{:S(2)}, u32[]{:S(2)}) async-start(bf16[64,16,180]{2,1,0:T(8,128)(2,1)} %copy.35), calls=%async_computation | async-start | bytes 1048576 | tf_op jit(solution)/shard_map/all_to_all | solution.py:81
  505.7 0.3 reduce_window_sum.17
  506.0 3.8 fusion.1
  509.8 1.8 fusion
  511.6 0.5 copy-done.7
  512.2 0.3 copy-done.8
  512.5 2.0 fusion.2
  514.5 19.3 %all-to-all-done = bf16[64,16,180]{2,1,0:T(8,128)(2,1)S(1)} async-done(((bf16[64,16,180]{2,1,0:T(8,128)(2,1)}), bf16[64,16,180]{2,1,0:T(8,128)(2,1)S(1)}, u32[]{:S(2)}, u32[]{:S(2)}) %all-to-all-start) | async-done | bytes 368672 | tf_op jit(solution)/shard_map/all_to_all | solution.py:81
  533.8 1.0 fusion.3
  (30 shorter events, 0.2 us)
Async XLA Ops:
  7.2 347.0 %copy-start = (bf16[1,1440,256]{2,1,0:T(8,128)(2,1)S(1)}, bf16[1,1440,256]{2,1,0:T(8,128)(2,1)}, u32[]{:S(2)}) copy-start(bf16[1,1440,256]{2,1,0:T(8,128)(2,1)} %param.15) | copy-start | bytes 2211844
  7.2 148.2 %all-gather.9.cloned.1.call-start = ((), (), s32[]{:S(2)}) async-start(), calls=%async_computation.2 | async-start | bytes 4259840 | tf_op jit(solution)/shard_map/all_gather | solution.py:58
  8.8 291.3 %all-gather.7.cloned.1.call-start = ((), (), s32[]{:S(2)}) async-start(), calls=%async_computation.1 | async-start | bytes 4259840 | tf_op jit(solution)/shard_map/all_gather | solution.py:59
  10.4 335.2 %all-gather.13.cloned.1.call-start = ((), (), s32[]{:S(2)}) async-start(), calls=%async_computation.4 | async-start | bytes 3391488 | tf_op jit(solution)/shard_map/all_gather | solution.py:69
  306.3 2.4 copy-start.5
  307.5 75.9 %all-gather.11.cloned.1.call-start = ((), (), s32[]{:S(2)}) async-start(), calls=%async_computation.3 | async-start | bytes 3391488 | tf_op jit(solution)/shard_map/all_gather | solution.py:70
  308.5 179.2 %all-reduce.3.cloned.1.call-start = ((), (), s32[]{:S(2)}) async-start(), calls=%async_computation.5 | async-start | bytes 6291456
  354.2 2.1 copy-start.2
  354.2 2.0 copy-start.4
  358.2 29.5 %copy-start.6 = (bf16[1,256,1440]{1,2,0:T(8,128)(2,1)S(1)}, bf16[1,256,1440]{1,2,0:T(8,128)(2,1)}, u32[]{:S(2)}) copy-start(bf16[1,256,1440]{1,2,0:T(8,128)(2,1)} %param.17) | copy-start | bytes 2211844
  490.1 43.7 %all-to-all-start = ((bf16[64,16,180]{2,1,0:T(8,128)(2,1)}), bf16[64,16,180]{2,1,0:T(8,128)(2,1)S(1)}, u32[]{:S(2)}, u32[]{:S(2)}) async-start(bf16[64,16,180]{2,1,0:T(8,128)(2,1)} %copy.35), calls=%async_computation | async-start | bytes 1048576 | tf_op jit(solution)/shard_map/all_to_all | solution.py:81
  506.0 3.8 copy-start.3
  509.8 1.8 copy-start.1
  509.8 2.4 copy-start.7
  509.8 2.7 copy-start.8
Sparse Core Ops, SparseCore 0:
  11.5 143.7 all-gather.8
  158.9 141.1 all-gather.6
  307.6 37.9 all-gather.12
  348.2 35.1 all-gather.10
  405.1 82.4 all-reduce.2
where the time goes:
time: 547 us; the launch traced here: 541 us
  waiting for transfers between devices  441 us (81%)
  local copies, waits for them, and re-layouts  42.1 us (8%)
  matrix products  20 us (4%)
  starting transfers between devices  16 us (3%)
  between operations  14.6 us (3%)
  other arithmetic  7.16 us (1%)
    all_gather x1, waiting for transfers between devices, on_device(): lax.all_gather(x_stash, 'expert', axis=0, tiled=True)  142 us
    all_gather x1, waiting for transfers between devices, on_device(): lax.all_gather(out_grad, 'expert', axis=0, tiled=True)  139 us
    unnamed x6, waiting for transfers between devices  80.1 us
    all_gather x1, waiting for transfers between devices, on_device(): lax.all_gather(picked_x, 'dp', axis=1, tiled=True)  36.4 us
    all_gather x1, waiting for transfers between devices, on_device(): lax.all_gather(picked_dy, 'dp', axis=1, tiled=True)  25.1 us
    all_to_all x1, waiting for transfers between devices, on_device(): lax.all_to_all(summed.astype(jnp.bfloat16), 'expert', split_axis=0, conca...  19.3 us
    all_to_all x1, starting transfers between devices, on_device(): lax.all_to_all(summed.astype(jnp.bfloat16), 'expert', split_axis=0, conca...  15.6 us
    unnamed x25, local copies, waits for them, and re-layouts  12.8 us
  transfers between devices with their start and end apart: 6, of which 6 were waited for; matrix products, arithmetic and copies ran while one was open for 6% of the time, Pallas kernels for 0%

commit v1 on v0

v1 whole, which is shorter than its diff:
```python
import jax
import jax.numpy as jnp
from jax import lax
from jax.experimental import pallas as pl
from jax.experimental.pallas import tpu as pltpu
from jax.sharding import PartitionSpec as P

TOP = 4
NX, NY, NZ = 4, 4, 16
CHUNKS = NZ // 2
TOK = 128
SLOTS = 16
FEAT = 180
WIDE = 384
HID = 256
HALF = NY * SLOTS
ROWS = 2 * HALF
LAG = 7
F32 = jnp.float32
BF16 = jnp.bfloat16


def kernel(
    tok, sel, gate, back_hot, w_gu, w_d, w_in,
    sum_out, ggu_out, gd_out,
    zp, zm, yb, g, dbuf, abuf, pb, sb, q, rl, rr, fl, fr, back, ret, fin,
    zp_s, zp_r, zm_s, zm_r, y_s, y_r, xr_s, xr_r, xl_s, xl_r, xfr_s, xfr_r, xfl_s, xfl_r,
    sib_s, sib_r, ps_s, ps_r, ar_s, ar_r, al_s, al_r, br_s, br_r, bl_s, bl_r,
    ret_s, ret0_s, ret_r, fin_s, fin_r,
):
    dp = lax.axis_index("dp")
    ex = lax.axis_index("expert")
    x, c = dp // 2, dp % 2
    z, y = ex // NY, ex % NY
    oc = 1 - c
    xr, xl, xo = (x + 1) % NX, (x + NX - 1) % NX, (x + 2) % NX

    def dev(x_, c_, y_, z_):
        return {"dp": x_ * 2 + c_, "expert": z_ * NY + y_}

    zright, zleft = dev(x, c, y, (z + 1) % NZ), dev(x, c, y, (z + NZ - 1) % NZ)
    xright, xleft = dev(xr, c, y, z), dev(xl, c, y, z)
    sibling = dev(x, oc, y, z)

    def ret_z(i):
        return jnp.where(c == 0, z + NZ - i, z + i + 1) % NZ

    def ret_from(i):
        return jnp.where(c == 0, z + i, z + NZ - i - 1) % NZ

    def rc(src, dst, s, r, to):
        return pltpu.make_async_remote_copy(
            src_ref=src, dst_ref=dst, send_sem=s, recv_sem=r, device_id=to,
            device_id_type=pl.DeviceIdType.MESH,
        )

    def take(ref, sem):
        pltpu.make_async_copy(ref, ref, sem).wait()

    barrier = pltpu.get_barrier_semaphore()
    for to in (zright, zleft, xright, xleft, sibling):
        pl.semaphore_signal(barrier, inc=1, device_id=to, device_id_type=pl.DeviceIdType.MESH)
    for d in range(1, NY):
        pl.semaphore_signal(
            barrier, inc=1, device_id=dev(x, c, (y + d) % NY, z),
            device_id_type=pl.DeviceIdType.MESH,
        )

    @pl.loop(0, CHUNKS)
    def _(i):
        for d in range(NY):
            def send_signal():
                pl.semaphore_signal(
                    barrier, inc=1, device_id=dev(x, c, (y + d) % NY, ret_from(i)),
                    device_id_type=pl.DeviceIdType.MESH,
                )

            if d == 0:
                pl.when((c == 1) | (i > 0))(send_signal)
            else:
                send_signal()

    pl.semaphore_wait(barrier, 8 + CHUNKS * NY - jnp.where(c == 0, 1, 0))

    def z_right(i):
        return rc(zp.at[i], zp.at[i + 1], zp_s.at[i], zp_r.at[i + 1], zright)

    def z_left(i):
        return rc(zm.at[i], zm.at[i + 1], zm_s.at[i], zm_r.at[i + 1], zleft)

    first_left = rc(tok, zm.at[0], zm_s.at[CHUNKS - 1], zm_r.at[0], zleft)
    first_right = rc(tok, zp.at[1], zp_s.at[0], zp_r.at[1], zright)
    first_left.start()
    first_right.start()
    zp[0] = tok[...]

    def slot_rows(which):
        return pl.ds(pl.multiple_of(which * SLOTS, SLOTS), SLOTS)

    def y_send(i, d):
        to = (y + d) % NY
        return rc(
            yb.at[i, :, slot_rows(to), :], g.at[c, x, i, :, slot_rows(y), :],
            y_s.at[i], y_r.at[i], dev(x, c, to, z),
        )

    def stage_z(i):
        take(zm.at[i], zm_r.at[i])

        @pl.when(i < CHUNKS - 1)
        def _():
            z_left(i).start()

        @pl.when(i > 0)
        def _():
            take(zp.at[i], zp_r.at[i])

            @pl.when(i < CHUNKS - 1)
            def _():
                z_right(i).start()

        for h, src in ((0, zp), (1, zm)):
            yb[i, h] = jnp.dot(sel[i, h], src[i], preferred_element_type=F32).astype(BF16)
        for d in range(1, NY):
            y_send(i, d).start()
        pltpu.make_async_copy(
            yb.at[i, :, slot_rows(y), :], g.at[c, x, i, :, slot_rows(y), :], y_r.at[i]
        ).start()

    def sib_send(i, x_):
        return rc(g.at[c, x_, i], g.at[c, x_, i], sib_s.at[i], sib_r.at[i], sibling)

    def x_right(i):
        return rc(g.at[c, x, i], g.at[c, x, i], xr_s.at[i], xr_r.at[i], xright)

    def x_left(i):
        return rc(g.at[c, x, i], g.at[c, x, i], xl_s.at[i], xl_r.at[i], xleft)

    def x_far_right(i):
        return rc(g.at[c, xl, i, 0], g.at[c, xl, i, 0], xfr_s.at[i], xfr_r.at[i], xright)

    def x_far_left(i):
        return rc(g.at[c, xr, i, 1], g.at[c, xr, i, 1], xfl_s.at[i], xfl_r.at[i], xleft)

    def stage_x1(i):
        take(g.at[c, x, i], y_r.at[i])
        x_right(i).start()
        x_left(i).start()
        sib_send(i, x).start()

    def stage_x2(i):
        take(g.at[c, xl, i], xr_r.at[i])
        x_far_right(i).start()
        take(g.at[c, xr, i], xl_r.at[i])
        x_far_left(i).start()
        sib_send(i, xl).start()
        sib_send(i, xr).start()

    def stage_x3(i):
        take(g.at[c, xo, i, 0], xfr_r.at[i])
        take(g.at[c, xo, i, 1], xfl_r.at[i])
        sib_send(i, xo).start()

    def p_send(i):
        return rc(pb.at[i, oc], sb.at[i], ps_s.at[i], ps_r.at[i], sibling)

    def stage_c(i):
        take(g.at[oc, :, i], sib_r.at[i])
        blocks = [g[c_, x_, i].reshape(ROWS, WIDE) for c_ in range(2) for x_ in range(NX)]
        low = jnp.concatenate([b[:, :HID] for b in blocks], axis=1)
        high = jnp.concatenate([b[:, WIDE - HID :] for b in blocks], axis=1)
        gu = jnp.dot(low, w_gu[...], preferred_element_type=F32)
        h = jnp.dot(high, w_d[...], preferred_element_type=F32)
        p = gate[i]
        gg, u = gu[:, :HID], gu[:, HID:]
        s = jax.nn.sigmoid(gg)
        gs = gg * s
        h = p * h
        abuf[i] = (p * gs * u).astype(BF16)
        d_gate = (h * u * s * (1.0 + gg * (1.0 - s))).astype(BF16)
        d_up = (h * gs).astype(BF16)
        dd = jnp.concatenate([d_gate, d_up], axis=1)
        dbuf[i] = dd
        for x_ in range(NX):
            piece = jnp.dot(dd, w_in[x_], preferred_element_type=F32).astype(BF16)
            pb[i, 0, x_] = piece[:HALF]
            pb[i, 1, x_] = piece[HALF:]
        p_send(i).start()

    quarter = HALF // 2

    def a_right(i):
        return rc(q.at[i, xo, pl.ds(0, quarter)], rl.at[i], ar_s.at[i], ar_r.at[i], xright)

    def a_left(i):
        return rc(q.at[i, xo, pl.ds(quarter, quarter)], rr.at[i], al_s.at[i], al_r.at[i], xleft)

    def b_right(i):
        return rc(q.at[i, xr], fl.at[i], br_s.at[i], br_r.at[i], xright)

    def b_left(i):
        return rc(q.at[i, xl], fr.at[i], bl_s.at[i], bl_r.at[i], xleft)

    def stage_r1(i):
        take(sb.at[i], ps_r.at[i])
        q[i] = (pb[i, c].astype(F32) + sb[i].astype(F32)).astype(BF16)
        a_right(i).start()
        a_left(i).start()

    def stage_r2(i):
        take(rl.at[i], ar_r.at[i])
        lo, hi = pl.ds(0, quarter), pl.ds(quarter, quarter)
        q[i, xr, lo] = (q[i, xr, lo].astype(F32) + rl[i].astype(F32)).astype(BF16)
        b_right(i).start()
        take(rr.at[i], al_r.at[i])
        q[i, xl, hi] = (q[i, xl, hi].astype(F32) + rr[i].astype(F32)).astype(BF16)
        b_left(i).start()

    def ret_send(i, d, sem):
        to = (y + d) % NY
        return rc(
            back.at[i, slot_rows(to), :], ret.at[i, slot_rows(y), :],
            sem, ret_r, dev(x, c, to, ret_z(i)),
        )

    def stage_r3(i):
        take(fl.at[i], br_r.at[i])
        take(fr.at[i], bl_r.at[i])
        back[i] = (q[i, x].astype(F32) + fl[i].astype(F32) + fr[i].astype(F32)).astype(BF16)
        for d in range(1, NY):
            ret_send(i, d, ret_s.at[i]).start()
        local = (c == 0) & (i == 0)

        @pl.when(local)
        def _():
            pltpu.make_async_copy(
                back.at[i, slot_rows(y), :], ret.at[i, slot_rows(y), :], ret_r
            ).start()

        @pl.when(jnp.logical_not(local))
        def _():
            ret_send(i, 0, ret0_s.at[i]).start()

    stages = (
        (stage_z, 0), (stage_x1, 1), (stage_x2, 2), (stage_x3, 3),
        (stage_c, 4), (stage_r1, 5), (stage_r2, 6), (stage_r3, 7),
    )

    @pl.loop(0, CHUNKS + LAG)
    def _(step):
        for stage, lag in stages:
            i = step - lag

            @pl.when((i >= 0) & (i < CHUNKS))
            def _():
                stage(i)

    first = (((0,), (0,)), ((), ()))
    rows = CHUNKS * ROWS

    @pl.loop(0, 2)
    def _(c_):
        @pl.loop(0, NX)
        def _(x_):
            own = g[c_, x_].reshape(rows, WIDE)
            dd = dbuf[...].reshape(rows, 2 * HID)
            ggu_out[x_, c_] = lax.dot_general(
                own[:, :HID], dd, first, preferred_element_type=F32
            )[: ggu_out.shape[2]].astype(BF16)
            aa = abuf[...].reshape(rows, HID)
            gd_out[x_, c_] = lax.dot_general(
                aa, own[:, WIDE - HID :], first, preferred_element_type=F32
            ).astype(BF16)

    take(ret, ret_r)
    fin[0] = jnp.dot(back_hot[...], ret[...].reshape(CHUNKS * HALF, WIDE), preferred_element_type=F32)
    last = rc(fin.at[0], fin.at[1], fin_s, fin_r, sibling)
    last.start()

    @pl.loop(0, CHUNKS)
    def _(i):
        @pl.when(i < CHUNKS - 1)
        def _():
            z_left(i).wait_send()
            z_right(i).wait_send()

        take(yb.at[i, :, pl.ds(0, (NY - 1) * SLOTS), :], y_s.at[i])
        x_right(i).wait_send()
        x_left(i).wait_send()
        x_far_right(i).wait_send()
        x_far_left(i).wait_send()
        take(g.at[c, :, i], sib_s.at[i])
        p_send(i).wait_send()
        a_right(i).wait_send()
        a_left(i).wait_send()
        b_right(i).wait_send()
        b_left(i).wait_send()
        take(back.at[i, pl.ds(0, (NY - 1) * SLOTS), :], ret_s.at[i])

        @pl.when((c == 1) | (i > 0))
        def _():
            ret_send(i, 0, ret0_s.at[i]).wait_send()

    first_left.wait_send()
    last.wait()
    sum_out[...] = fin[0] + fin[1]


def one_hot(hit, tri):
    rank = jnp.dot(hit.astype(BF16), tri, preferred_element_type=F32).astype(jnp.int32)
    slot = lax.broadcasted_iota(jnp.int32, (SLOTS, 1), 0)
    return (rank[..., None, :] == slot) & hit[..., None, :]


def on_device(x_stash, out_grad, expert_ids, gates, scales, w_gate, w_up, w_down):
    dp = lax.axis_index("dp")
    ex = lax.axis_index("expert")
    c = dp % 2
    z, y = ex // NY, ex % NY

    scale = lax.dynamic_slice_in_dim(scales, ex * TOK, TOK, 0)
    xs = (x_stash.astype(F32) * scale[:, None]).astype(BF16)
    tok = jnp.concatenate([xs, out_grad, jnp.zeros((TOK, WIDE - 2 * FEAT), BF16)], axis=1)

    tri = (
        lax.broadcasted_iota(jnp.int32, (TOK, TOK), 0)
        < lax.broadcasted_iota(jnp.int32, (TOK, TOK), 1)
    ).astype(BF16)

    def relative(a):
        a = a.reshape(TOP, NZ, NY, TOK)
        a = jnp.concatenate([a, a], axis=1)
        low = lax.dynamic_slice_in_dim(a, z + NZ - CHUNKS + 1, CHUNKS, 1)[:, ::-1]
        high = lax.dynamic_slice_in_dim(a, z + 1, CHUNKS, 1)
        return jnp.stack([low, high], axis=2)

    ids = relative(expert_ids)
    weights = relative(gates)
    ids_y = lax.dynamic_index_in_dim(ids, y, 3, keepdims=False)
    experts = z * NY + jnp.arange(NY, dtype=jnp.int32)
    hit = jnp.any(ids_y[:, :, :, None, :] == experts[:, None], axis=0)
    sel = one_hot(hit, tri).astype(BF16).reshape(CHUNKS, 2, HALF, TOK)
    named = ids == ex
    weight = jnp.sum(jnp.where(named, weights, F32(0.0)), axis=0)
    mine = one_hot(jnp.any(named, axis=0), tri)
    gate = jnp.sum(jnp.where(mine, weight[..., None, :], F32(0.0)), axis=-1)
    gate = gate.reshape(CHUNKS, ROWS, 1)

    own_ids = lax.dynamic_slice_in_dim(expert_ids, ex * TOK, TOK, 1)
    step = jnp.arange(CHUNKS, dtype=jnp.int32)
    from_z = jnp.where(c == 0, z + step, z + NZ - 1 - step) % NZ
    senders = from_z[:, None] * NY + jnp.arange(NY, dtype=jnp.int32)
    sent = jnp.any(own_ids[:, None, None, :] == senders[:, :, None], axis=0)
    back_hot = one_hot(sent, tri).astype(BF16).reshape(CHUNKS * HALF, TOK).T

    def by_owner(w):
        w = w.reshape(NX, 2, FEAT, HID).transpose(1, 0, 2, 3)
        return jnp.pad(w, ((0, 0), (0, 0), (0, HID - FEAT), (0, 0))).reshape(2 * NX * HID, HID)

    w_gu = jnp.concatenate([by_owner(w_gate[0]), by_owner(w_up[0])], axis=1)
    shift = FEAT - (WIDE - HID)
    w_d = w_down[0].T.reshape(NX, 2, FEAT, HID).transpose(1, 0, 2, 3)
    w_d = jnp.pad(w_d, ((0, 0), (0, 0), (shift, HID - FEAT - shift), (0, 0)))
    w_d = w_d.reshape(2 * NX * HID, HID)

    def by_chip(w):
        w = w.reshape(NX, 2 * FEAT, HID).transpose(0, 2, 1)
        return jnp.pad(w, ((0, 0), (0, 0), (0, WIDE - 2 * FEAT)))

    w_in = jnp.concatenate([by_chip(w_gate[0]), by_chip(w_up[0])], axis=1)

    vmem = pl.BlockSpec(memory_space=pltpu.VMEM)
    keep = 192
    block = (CHUNKS, 2, HALF, WIDE)
    dma = pltpu.SemaphoreType.DMA
    per_chunk = dma((CHUNKS,))
    total, ggu, gd = pl.pallas_call(
        kernel,
        out_shape=(
            jax.ShapeDtypeStruct((TOK, WIDE), F32),
            jax.ShapeDtypeStruct((NX, 2, keep, 2 * HID), BF16),
            jax.ShapeDtypeStruct((NX, 2, HID, HID), BF16),
        ),
        in_specs=[vmem] * 7,
        out_specs=(vmem, vmem, vmem),
        scratch_shapes=[
            pltpu.VMEM((CHUNKS, TOK, WIDE), BF16),
            pltpu.VMEM((CHUNKS, TOK, WIDE), BF16),
            pltpu.VMEM(block, BF16),
            pltpu.VMEM((2, NX) + block, BF16),
            pltpu.VMEM((CHUNKS, ROWS, 2 * HID), BF16),
            pltpu.VMEM((CHUNKS, ROWS, HID), BF16),
            pltpu.VMEM((CHUNKS, 2, NX, HALF, WIDE), BF16),
            pltpu.VMEM((CHUNKS, NX, HALF, WIDE), BF16),
            pltpu.VMEM((CHUNKS, NX, HALF, WIDE), BF16),
            pltpu.VMEM((CHUNKS, HALF // 2, WIDE), BF16),
            pltpu.VMEM((CHUNKS, HALF // 2, WIDE), BF16),
            pltpu.VMEM((CHUNKS, HALF, WIDE), BF16),
            pltpu.VMEM((CHUNKS, HALF, WIDE), BF16),
            pltpu.VMEM((CHUNKS, HALF, WIDE), BF16),
            pltpu.VMEM((CHUNKS, HALF, WIDE), BF16),
            pltpu.VMEM((2, TOK, WIDE), F32),
        ]
        + [per_chunk] * 26
        + [per_chunk, per_chunk, dma, dma, dma],
        compiler_params=pltpu.CompilerParams(
            collective_id=0, has_side_effects=True, vmem_limit_bytes=56 * 1024 * 1024
        ),
    )(tok, sel, gate, back_hot, w_gu, w_d, w_in)

    grad_input = lax.dynamic_slice_in_dim(total, c * FEAT, FEAT, 1).astype(BF16)
    d = 2 * NX * FEAT
    grad_gate = ggu[:, :, :FEAT, :HID].reshape(d, HID)
    grad_up = ggu[:, :, :FEAT, HID:].reshape(d, HID)
    grad_down = gd[:, :, :, shift : shift + FEAT].transpose(2, 0, 1, 3).reshape(HID, d)
    return grad_input, grad_gate[None], grad_up[None], grad_down[None]


def solution(mesh):
    return jax.shard_map(
        on_device,
        mesh=mesh,
        in_specs=(
            P("expert", "dp"),
            P("expert", "dp"),
            P(),
            P(),
            P(),
            P("expert", None, "dp"),
            P("expert", None, "dp"),
            P("expert", "dp", None),
        ),
        out_specs=(
            P("expert", "dp"),
            P("expert", None, "dp"),
            P("expert", None, "dp"),
            P("expert", "dp", None),
        ),
        check_vma=False,
    )
```

time: 547 us -> 122 us (0.22)
  waiting for transfers between devices: 441 us -> 0 us
  Pallas kernels: 0 us -> 96.6 us
  local copies, waits for them, and re-layouts: 42.1 us -> 17.6 us
  matrix products: 20 us -> 0.41 us
  starting transfers between devices: 16 us -> 0 us
  between operations: 14.6 us -> 0.99 us
    all_gather x4 -> x0, waiting for transfers between devices: 342 us -> none  [the longest x1 142 us: on_device(): lax.all_gather(x_stash, 'expert', axis=0, tiled=True)]
    pallas_call x0 -> x1, Pallas kernels: none -> 96.6 us  [on_device(): pl.pallas_call(kernel, out_shape=(jax.ShapeDtypeStruct((TOK, WIDE), F32),...]
    unnamed x6 -> x0, waiting for transfers between devices: 80.1 us -> none
    dot_general x9 -> x3, matrix products: 20 us -> 0.41 us  [one_hot(): jnp.dot(hit.astype(BF16), tri, preferred_element_type=F32).astype(jnp.int32)]
    all_to_all x1 -> x0, waiting for transfers between devices: 19.3 us -> none  [on_device(): lax.all_to_all(summed.astype(jnp.bfloat16), 'expert', split_axis=0, conca...]
    all_to_all x1 -> x0, starting transfers between devices: 15.6 us -> none  [on_device(): lax.all_to_all(summed.astype(jnp.bfloat16), 'expert', split_axis=0, conca...]
    gather x2 -> x0, local copies, waits for them, and re-layouts: 12.4 us -> none  [the longest x1 6.19 us: on_device(): picked_x = jnp.take(every_x, rows, axis=0)]
    unnamed x25 -> x15, local copies, waits for them, and re-layouts: 12.8 us -> 2.64 us
  transfers between devices with their start and end apart: 6 -> 0, of which waited for: 6 -> 0; matrix products, arithmetic and copies ran while one was open for 6% -> 0% of each run, Pallas kernels for 0% -> 0%
where the time goes in v1:
time: 122 us; the launch traced here: 121 us
  Pallas kernels  96.6 us (79%)
  local copies, waits for them, and re-layouts  17.6 us (14%)
  other arithmetic  5.84 us (5%)
    pallas_call x1, Pallas kernels, on_device(): pl.pallas_call(kernel, out_shape=(jax.ShapeDtypeStruct((TOK, WIDE), F32),...  96.6 us
    another operation x3, local copies, waits for them, and re-layouts, on_device(): return (grad_input, grad_gate[None], grad_up[None], grad_down[None])  2.98 us
    unnamed x15, local copies, waits for them, and re-layouts  2.64 us

profile of v1, /device:TPU:1, one launch (start us, length us, event | category | flops | bytes accessed | tf_op | source)
XLA Modules:
  0.0 121.5 jit_solution(3789260194381022805)
XLA Ops:
  0.7 0.8 dynamic_slice.25
  1.5 0.1 pad.33.clone
  1.6 0.7 constant_dynamic-slice_fusion
  2.3 0.1 compare_reduce_fusion.1
  2.3 0.1 eq.102
  2.4 0.1 convolution_convert_fusion.2
  2.6 0.1 eq.117
  2.7 0.2 copy.118
  2.9 0.9 copy.107
  3.8 1.0 reshape.93
  4.8 1.0 reshape.92
  5.8 0.9 copy.106
  6.7 0.1 multiply_convert_fusion
  6.8 0.7 maximum_maximum_fusion.tok
  7.6 0.1 copy.116
  7.7 0.0 copy-start.3
  7.7 0.7 fusion.7.back_hot
  8.6 0.1 fusion.18
  8.6 0.1 compare_reduce_fusion
  8.8 0.1 convolution_convert_fusion.1
  8.9 0.1 convolution_convert_fusion
  9.1 0.9 fusion.5.sel
  10.0 0.1 fusion.8
  10.1 0.2 select_reduce_fusion
  10.3 1.1 reshape.101.gate
  11.5 0.1 reshape.97
  11.6 0.1 copy.130
  11.6 1.2 %pad.20.clone = bf16[2,4,256,256]{3,2,1,0:T(8,128)(2,1)} pad(bf16[2,4,180,256]{3,2,1,0:T(8,128)(2,1)S(1)} %copy.130, bf16[]{:T(256)} %constant.75.clone.1), padding=0_0x0_0x52_24x0_0 | pad | bytes 1785858 | tf_op jit(solution)/shard_map/jit(_pad)/pad | solution.py:363
  12.9 0.1 reshape_squeeze.12
  13.0 0.1 copy.128
  13.1 0.1 pad.18.clone
  13.2 0.8 copy-done
  14.0 0.1 reshape_squeeze.13
  14.1 0.1 copy.129
  14.2 0.1 pad.19.clone
  14.3 1.5 %pad_maximum_fusion.w_gu = bf16[2048,512]{1,0:T(8,128)(2,1)} fusion(bf16[2048,256]{1,0:T(8,128)(2,1)S(1)} %bitcast.53, bf16[2048,256]{1,0:T(8,128)(2,1)S(1)} %bitcast.52), kind=kLoop, calls=%fused_computation.4 | loop fusion | flops 4194304 | bytes 4194304 | tf_op jit(solution)/shard_map/concatenate | solution.py:360
  15.8 0.4 copy.123
  16.1 0.4 copy.122
  16.5 1.3 %fusion.2.w_in = bf16[4,512,384]{2,1,0:T(8,128)(2,1)} fusion(bf16[4,256,360]{2,1,0:T(8,128)(2,1)S(1)} %bitcast.54, bf16[4,256,360]{2,1,0:T(8,128)(2,1)S(1)} %bitcast.55), kind=kLoop, calls=%fused_computation.5 | loop fusion | flops 6291456 | bytes 3047424 | tf_op jit(solution)/shard_map/concatenate | solution.py:370
  17.8 96.6 %shard_map.111 = (f32[128,384]{1,0:T(8,128)}, bf16[4,2,192,512]{3,2,1,0:T(8,128)(2,1)}, bf16[4,2,256,256]{3,2,1,0:T(8,128)(2,1)}) custom-call(bf16[128,384]{1,0:T(8,128)(2,1)} %maximum_maximum_fusion.tok, bf16[8,2,64,128]{3,2,1,0:T(8,128)(2,1)} %fusion.5.sel, f32[8,128,1]{2,1,0:T(8,128)} %reshape.101.gate, bf16[128,512]{1,0:T(8,128)(2,1)} %fusion.7.back_hot, ...), custom_call_target="tpu_custom_call" | custom-call | tf_op jit(solution)/shard_map/pallas_call | solution.py:377
  114.4 1.0 dynamic-slice_convert_fusion
  115.4 0.7 copy.126
  116.2 1.7 %slice_bitcast_fusion = bf16[256,4,2,180]{3,0,2,1:T(8,128)(2,1)S(1)} fusion(bf16[4,2,256,256]{3,2,1,0:T(8,128)(2,1)} %get-tuple-element.9), kind=kLoop, calls=%fused_computation.9 | loop fusion | bytes 1474560 | tf_op jit(solution)/shard_map/transpose | solution.py:415
  117.8 0.5 copy.125
  118.4 1.0 broadcast_in_dim_reshape.11
  119.4 0.1 fusion.20
  119.5 1.0 broadcast_in_dim_reshape.10
  120.5 1.0 broadcast_in_dim_reshape.9
  (29 shorter events, 0.3 us)
Async XLA Ops:
  7.7 3.8 %copy-start.3 = (bf16[1,256,1440]{1,2,0:T(8,128)(2,1)S(1)}, bf16[1,256,1440]{1,2,0:T(8,128)(2,1)}, u32[]{:S(2)}) copy-start(bf16[1,256,1440]{1,2,0:T(8,128)(2,1)} %param.15) | copy-start | bytes 2211844
  11.5 1.4 %copy-start.1 = (bf16[1,1440,256]{2,1,0:T(8,128)(2,1)S(1)}, bf16[1,1440,256]{2,1,0:T(8,128)(2,1)}, u32[]{:S(2)}) copy-start(bf16[1,1440,256]{2,1,0:T(8,128)(2,1)} %param.13) | copy-start | bytes 2211844
  12.9 1.1 copy-start
  117.8 1.5 %copy-start.2 = (bf16[4,2,192,512]{3,2,1,0:T(8,128)(2,1)S(1)}, bf16[4,2,192,512]{3,2,1,0:T(8,128)(2,1)}, u32[]{:S(2)}) copy-start(bf16[4,2,192,512]{3,2,1,0:T(8,128)(2,1)} %get-tuple-element.8) | copy-start | bytes 4718596

commit v2 on v1

v2 whole, which is shorter than its diff:
```python
import jax
import jax.numpy as jnp
from jax import lax
from jax.experimental import pallas as pl
from jax.experimental.pallas import tpu as pltpu
from jax.sharding import PartitionSpec as P

TOP = 4
NX, NY, NZ = 4, 4, 16
CHUNKS = NZ // 2
TOK = 128
SLOTS = 16
FEAT = 180
WIDE = 384
HID = 256
HALF = NY * SLOTS
ROWS = 2 * HALF
LAG = 7
F32 = jnp.float32
BF16 = jnp.bfloat16


def one_hot(hit, rows):
    tri = (
        lax.broadcasted_iota(jnp.int32, (TOK, TOK), 0)
        < lax.broadcasted_iota(jnp.int32, (TOK, TOK), 1)
    ).astype(BF16)
    rank = jnp.dot(hit.astype(BF16), tri, preferred_element_type=F32)
    code = jnp.where(hit > 0.0, rank, F32(-1.0))
    code = jnp.broadcast_to(code[:, None, :], (rows, SLOTS, TOK)).reshape(rows * SLOTS, TOK)
    slot = lax.broadcasted_iota(jnp.int32, (rows * SLOTS, TOK), 0) & (SLOTS - 1)
    return code == slot.astype(F32)


def far(i):
    return (i >> 1) + (CHUNKS // 2) * (i & 1)


def kernel(
    x_in, dy_in, ids, gates, scales, wg_hbm, wu_hbm, wd_hbm,
    gi_out, gg_out, gu_out, gd_out,
    wg, wu, wdt, w_in, sel, gate, xs_buf, dy_buf,
    zp, zm, yb, g, dgbuf, dubuf, abuf, pb, sb, q, rl, rr, fl, fr, back, ret, fin,
    w_sem, zp_s, zp_r, zm_s, zm_r, y_s, y_r, xr_s, xr_r, xl_s, xl_r, xfr_s, xfr_r, xfl_s, xfl_r,
    sib_s, sib_r, ps_s, ps_r, ar_s, ar_r, al_s, al_r, br_s, br_r, bl_s, bl_r,
    ret_s, ret0_s, ret_r, fin_s, fin_r,
):
    dp = lax.axis_index("dp")
    ex = lax.axis_index("expert")
    x, c = dp // 2, dp % 2
    z, y = ex // NY, ex % NY
    oc = 1 - c
    xr, xl, xo = (x + 1) % NX, (x + NX - 1) % NX, (x + 2) % NX

    def dev(x_, c_, y_, z_):
        return {"dp": x_ * 2 + c_, "expert": z_ * NY + y_}

    zright, zleft = dev(x, c, y, (z + 1) % NZ), dev(x, c, y, (z + NZ - 1) % NZ)
    xright, xleft = dev(xr, c, y, z), dev(xl, c, y, z)
    sibling = dev(x, oc, y, z)

    def ret_z(i):
        return jnp.where(c == 0, z + NZ - far(i), z + far(i) + 1) % NZ

    def ret_from(i):
        return jnp.where(c == 0, z + far(i), z + NZ - far(i) - 1) % NZ

    def rc(src, dst, s, r, to):
        return pltpu.make_async_remote_copy(
            src_ref=src, dst_ref=dst, send_sem=s, recv_sem=r, device_id=to,
            device_id_type=pl.DeviceIdType.MESH,
        )

    def take(ref, sem):
        pltpu.make_async_copy(ref, ref, sem).wait()

    jump = CHUNKS // 2
    express_right = dev(x, c, y, (z + jump) % NZ)
    express_left = dev(x, c, y, (z + NZ - jump - 1) % NZ)
    weights = [
        pltpu.make_async_copy(src, dst, w_sem.at[n])
        for n, (src, dst) in enumerate(((wg_hbm, wg), (wu_hbm, wu), (wd_hbm, wdt)))
    ]
    for copy in weights:
        copy.start()

    barrier = pltpu.get_barrier_semaphore()
    for to in (
        zright, zleft, xright, xleft, sibling,
        dev(x, c, y, (z + NZ - jump) % NZ), dev(x, c, y, (z + jump + 1) % NZ),
    ):
        pl.semaphore_signal(barrier, inc=1, device_id=to, device_id_type=pl.DeviceIdType.MESH)
    for d in range(1, NY):
        pl.semaphore_signal(
            barrier, inc=1, device_id=dev(x, c, (y + d) % NY, z),
            device_id_type=pl.DeviceIdType.MESH,
        )

    @pl.loop(0, CHUNKS)
    def _(i):
        for d in range(NY):
            def send_signal():
                pl.semaphore_signal(
                    barrier, inc=1, device_id=dev(x, c, (y + d) % NY, ret_from(i)),
                    device_id_type=pl.DeviceIdType.MESH,
                )

            if d == 0:
                pl.when((c == 1) | (i > 0))(send_signal)
            else:
                send_signal()

    xs_own = (x_in[...].astype(F32) * scales[pl.ds(ex, 1), :]).astype(BF16).astype(F32)
    own = [xs_own, dy_in[...].astype(F32), jnp.zeros((WIDE - 2 * FEAT, TOK), F32)]
    zp[0] = jnp.concatenate(own, axis=0).astype(BF16).T

    pl.semaphore_wait(barrier, 10 + CHUNKS * NY - jnp.where(c == 0, 1, 0))

    def z_right(i):
        return rc(zp.at[i], zp.at[i + 2], zp_s.at[i], zp_r.at[i + 2], zright)

    def z_left(i):
        return rc(zm.at[i], zm.at[i + 2], zm_s.at[i], zm_r.at[i + 2], zleft)

    first = (
        rc(zp.at[0], zp.at[2], zp_s.at[0], zp_r.at[2], zright),
        rc(zp.at[0], zm.at[0], zm_s.at[CHUNKS - 1], zm_r.at[0], zleft),
        rc(zp.at[0], zp.at[1], zp_s.at[CHUNKS - 1], zp_r.at[1], express_right),
        rc(zp.at[0], zm.at[1], zm_s.at[CHUNKS - 2], zm_r.at[1], express_left),
    )
    for copy in first:
        copy.start()

    def origins(i):
        return (z + NZ - far(i)) % NZ, (z + far(i) + 1) % NZ

    def prepare_sel(i):
        expert = z * NY + lax.broadcasted_iota(jnp.int32, (NY, TOK), 0)
        hits = []
        for zo in origins(i):
            block = ids[zo * NY + y]
            hit = jnp.zeros((NY, TOK), F32)
            for k in range(TOP):
                hit = hit + jnp.where(block[k : k + 1] == expert, F32(1.0), F32(0.0))
            hits.append(hit)
        hot = one_hot(jnp.concatenate(hits, axis=0), 2 * NY)
        sel[i] = jnp.where(hot, F32(1.0), F32(0.0)).astype(BF16)

    def prepare_gate(i):
        hits, weight = [], []
        for zo in origins(i):
            for ys in range(NY):
                named = ids[zo * NY + ys] == ex
                hits.append(jnp.sum(jnp.where(named, F32(1.0), F32(0.0)), axis=0, keepdims=True))
                weight.append(
                    jnp.sum(
                        jnp.where(named, gates[zo * NY + ys], F32(0.0)), axis=0, keepdims=True
                    )
                )
        hot = one_hot(jnp.concatenate(hits, axis=0), 2 * NY)
        w = jnp.concatenate(weight, axis=0)
        w = jnp.broadcast_to(w[:, None, :], (2 * NY, SLOTS, TOK)).reshape(ROWS, TOK)
        gate[i] = jnp.sum(jnp.where(hot, w, F32(0.0)), axis=1, keepdims=True)

    pl.loop(0, CHUNKS)(prepare_sel)

    def slot_rows(which):
        return pl.ds(pl.multiple_of(which * SLOTS, SLOTS), SLOTS)

    def y_send(i, d):
        to = (y + d) % NY
        return rc(
            yb.at[i, :, slot_rows(to), :], g.at[c, x, i, :, slot_rows(y), :],
            y_s.at[i], y_r.at[i], dev(x, c, to, z),
        )

    def stage_z(i):
        take(zm.at[i], zm_r.at[i])

        @pl.when(i < CHUNKS - 2)
        def _():
            z_left(i).start()

        @pl.when(i > 0)
        def _():
            take(zp.at[i], zp_r.at[i])

            @pl.when(i < CHUNKS - 2)
            def _():
                z_right(i).start()

        for h, src in ((0, zp), (1, zm)):
            yb[i, h] = jnp.dot(
                sel[i, pl.ds(h * HALF, HALF)], src[i], preferred_element_type=F32
            ).astype(BF16)
        for d in range(1, NY):
            y_send(i, d).start()
        pltpu.make_async_copy(
            yb.at[i, :, slot_rows(y), :], g.at[c, x, i, :, slot_rows(y), :], y_r.at[i]
        ).start()

    def sib_send(i, x_):
        return rc(g.at[c, x_, i], g.at[c, x_, i], sib_s.at[i], sib_r.at[i], sibling)

    def x_right(i):
        return rc(g.at[c, x, i], g.at[c, x, i], xr_s.at[i], xr_r.at[i], xright)

    def x_left(i):
        return rc(g.at[c, x, i], g.at[c, x, i], xl_s.at[i], xl_r.at[i], xleft)

    def x_far_right(i):
        return rc(g.at[c, xl, i, 0], g.at[c, xl, i, 0], xfr_s.at[i], xfr_r.at[i], xright)

    def x_far_left(i):
        return rc(g.at[c, xr, i, 1], g.at[c, xr, i, 1], xfl_s.at[i], xfl_r.at[i], xleft)

    def stage_x1(i):
        take(g.at[c, x, i], y_r.at[i])
        x_right(i).start()
        x_left(i).start()
        sib_send(i, x).start()

    def stage_x2(i):
        take(g.at[c, xl, i], xr_r.at[i])
        x_far_right(i).start()
        take(g.at[c, xr, i], xl_r.at[i])
        x_far_left(i).start()
        sib_send(i, xl).start()
        sib_send(i, xr).start()

    def stage_x3(i):
        take(g.at[c, xo, i, 0], xfr_r.at[i])
        take(g.at[c, xo, i, 1], xfl_r.at[i])
        sib_send(i, xo).start()

    def p_send(i):
        return rc(pb.at[i, oc], sb.at[i], ps_s.at[i], ps_r.at[i], sibling)

    def stage_c(i):
        take(g.at[oc, :, i], sib_r.at[i])
        blocks = [g[c_, x_, i].reshape(ROWS, WIDE) for x_ in range(NX) for c_ in range(2)]
        xs = jnp.concatenate([b[:, :FEAT] for b in blocks], axis=1)
        dys = jnp.concatenate([b[:, FEAT : 2 * FEAT] for b in blocks], axis=1)
        xs_buf[i] = xs
        dy_buf[i] = dys
        gg = jnp.dot(xs, wg[...], preferred_element_type=F32)
        u = jnp.dot(xs, wu[...], preferred_element_type=F32)
        h = jnp.dot(dys, wdt[...], preferred_element_type=F32)
        p = gate[i]
        s = jax.nn.sigmoid(gg)
        gs = gg * s
        h = p * h
        abuf[i] = (p * gs * u).astype(BF16)
        d_gate = (h * u * s * (1.0 + gg * (1.0 - s))).astype(BF16)
        d_up = (h * gs).astype(BF16)
        dgbuf[i] = d_gate
        dubuf[i] = d_up
        dd = jnp.concatenate([d_gate, d_up], axis=1)
        for x_ in range(NX):
            piece = jnp.dot(dd, w_in[x_], preferred_element_type=F32).astype(BF16)
            pb[i, 0, x_] = piece[:HALF]
            pb[i, 1, x_] = piece[HALF:]
        p_send(i).start()

    quarter = HALF // 2

    def a_right(i):
        return rc(q.at[i, xo, pl.ds(0, quarter)], rl.at[i], ar_s.at[i], ar_r.at[i], xright)

    def a_left(i):
        return rc(q.at[i, xo, pl.ds(quarter, quarter)], rr.at[i], al_s.at[i], al_r.at[i], xleft)

    def b_right(i):
        return rc(q.at[i, xr], fl.at[i], br_s.at[i], br_r.at[i], xright)

    def b_left(i):
        return rc(q.at[i, xl], fr.at[i], bl_s.at[i], bl_r.at[i], xleft)

    def stage_r1(i):
        take(sb.at[i], ps_r.at[i])
        q[i] = (pb[i, c].astype(F32) + sb[i].astype(F32)).astype(BF16)
        a_right(i).start()
        a_left(i).start()

    def stage_r2(i):
        take(rl.at[i], ar_r.at[i])
        lo, hi = pl.ds(0, quarter), pl.ds(quarter, quarter)
        q[i, xr, lo] = (q[i, xr, lo].astype(F32) + rl[i].astype(F32)).astype(BF16)
        b_right(i).start()
        take(rr.at[i], al_r.at[i])
        q[i, xl, hi] = (q[i, xl, hi].astype(F32) + rr[i].astype(F32)).astype(BF16)
        b_left(i).start()

    def ret_send(i, d, sem):
        to = (y + d) % NY
        return rc(
            back.at[i, slot_rows(to), :], ret.at[i, slot_rows(y), :],
            sem, ret_r, dev(x, c, to, ret_z(i)),
        )

    def stage_r3(i):
        take(fl.at[i], br_r.at[i])
        take(fr.at[i], bl_r.at[i])
        back[i] = (q[i, x].astype(F32) + fl[i].astype(F32) + fr[i].astype(F32)).astype(BF16)
        for d in range(1, NY):
            ret_send(i, d, ret_s.at[i]).start()
        local = (c == 0) & (i == 0)

        @pl.when(local)
        def _():
            pltpu.make_async_copy(
                back.at[i, slot_rows(y), :], ret.at[i, slot_rows(y), :], ret_r
            ).start()

        @pl.when(jnp.logical_not(local))
        def _():
            ret_send(i, 0, ret0_s.at[i]).start()

    stages = (
        (stage_z, 0), (stage_x1, 1), (stage_x2, 2), (stage_x3, 3),
        (stage_c, 4), (stage_r1, 5), (stage_r2, 6), (stage_r3, 7),
    )

    def prepare_in():
        for copy in weights:
            copy.wait()
        for n, w in enumerate((wg, wu)):
            wide = jnp.concatenate(
                [w[...].astype(F32), jnp.zeros((WIDE - 2 * FEAT, HID), F32)], axis=0
            )
            for x_ in range(NX):
                rows = wide[2 * FEAT * x_ : 2 * FEAT * x_ + WIDE].astype(BF16)
                w_in[x_, n * HID : (n + 1) * HID] = rows.T

    over_rows = (((0,), (0,)), ((), ()))

    def flat(ref):
        return ref[...].reshape(CHUNKS * ROWS, ref.shape[-1])

    def over_slots(a, b, out):
        out[...] = lax.dot_general(
            flat(a), flat(b), over_rows, preferred_element_type=F32
        ).astype(BF16)

    extra = {
        0: lambda: pl.loop(0, CHUNKS)(prepare_gate),
        1: prepare_in,
        CHUNKS + LAG - 3: lambda: over_slots(xs_buf, dgbuf, gg_out),
        CHUNKS + LAG - 2: lambda: over_slots(xs_buf, dubuf, gu_out),
        CHUNKS + LAG - 1: lambda: over_slots(dy_buf, abuf, gd_out),
    }

    @pl.loop(0, CHUNKS + LAG)
    def _(step):
        for stage, lag in stages:
            i = step - lag

            @pl.when((i >= 0) & (i < CHUNKS))
            def _():
                stage(i)

        for at, work in extra.items():
            pl.when(step == at)(work)

    order = lax.broadcasted_iota(jnp.int32, (CHUNKS * NY, TOK), 0)
    step_of, y_of = order >> 2, order & (NY - 1)
    dist = far(step_of)
    from_z = jnp.where(c == 0, z + dist, z + NZ - 1 - dist) & (NZ - 1)
    sender = from_z * NY + y_of
    own = ids[ex]
    hit = jnp.zeros((CHUNKS * NY, TOK), F32)
    for k in range(TOP):
        hit = hit + jnp.where(own[k : k + 1] == sender, F32(1.0), F32(0.0))
    back_hot = jnp.where(one_hot(hit, CHUNKS * NY), F32(1.0), F32(0.0)).astype(BF16)
    take(ret, ret_r)
    fin[0] = lax.dot_general(
        ret[...].reshape(CHUNKS * HALF, WIDE), back_hot, over_rows, preferred_element_type=F32
    )
    last = rc(fin.at[0], fin.at[1], fin_s, fin_r, sibling)
    last.start()

    @pl.loop(0, CHUNKS)
    def _(i):
        @pl.when(i < CHUNKS - 2)
        def _():
            z_left(i).wait_send()

            @pl.when(i > 0)
            def _():
                z_right(i).wait_send()

        take(yb.at[i, :, pl.ds(0, (NY - 1) * SLOTS), :], y_s.at[i])
        x_right(i).wait_send()
        x_left(i).wait_send()
        x_far_right(i).wait_send()
        x_far_left(i).wait_send()
        take(g.at[c, :, i], sib_s.at[i])
        p_send(i).wait_send()
        a_right(i).wait_send()
        a_left(i).wait_send()
        b_right(i).wait_send()
        b_left(i).wait_send()
        take(back.at[i, pl.ds(0, (NY - 1) * SLOTS), :], ret_s.at[i])

        @pl.when((c == 1) | (i > 0))
        def _():
            ret_send(i, 0, ret0_s.at[i]).wait_send()

    for copy in first:
        copy.wait_send()
    last.wait()
    total = fin[0] + fin[1]
    gi_out[...] = jnp.where(c == 0, total[:FEAT], total[FEAT : 2 * FEAT]).astype(BF16)


def on_device(x_stash, out_grad, expert_ids, gates, scales, w_gate, w_up, w_down):
    blocks = NZ * NY
    d = 2 * NX * FEAT

    def by_block(a):
        return a.reshape(TOP, blocks, TOK).transpose(1, 0, 2)

    vmem = pl.BlockSpec(memory_space=pltpu.VMEM)
    hbm = pl.BlockSpec(memory_space=pl.ANY)
    block = (CHUNKS, 2, HALF, WIDE)
    dma = pltpu.SemaphoreType.DMA
    per_chunk = dma((CHUNKS,))
    grad_input, grad_gate, grad_up, grad_down = pl.pallas_call(
        kernel,
        out_shape=(
            jax.ShapeDtypeStruct((FEAT, TOK), BF16),
            jax.ShapeDtypeStruct((d, HID), BF16),
            jax.ShapeDtypeStruct((d, HID), BF16),
            jax.ShapeDtypeStruct((d, HID), BF16),
        ),
        in_specs=[vmem] * 5 + [hbm] * 3,
        out_specs=(vmem,) * 4,
        scratch_shapes=[
            pltpu.VMEM((d, HID), BF16),
            pltpu.VMEM((d, HID), BF16),
            pltpu.VMEM((d, HID), BF16),
            pltpu.VMEM((NX, 2 * HID, WIDE), BF16),
            pltpu.VMEM((CHUNKS, ROWS, TOK), BF16),
            pltpu.VMEM((CHUNKS, ROWS, 1), F32),
            pltpu.VMEM((CHUNKS, ROWS, d), BF16),
            pltpu.VMEM((CHUNKS, ROWS, d), BF16),
            pltpu.VMEM((CHUNKS, TOK, WIDE), BF16),
            pltpu.VMEM((CHUNKS, TOK, WIDE), BF16),
            pltpu.VMEM(block, BF16),
            pltpu.VMEM((2, NX) + block, BF16),
            pltpu.VMEM((CHUNKS, ROWS, HID), BF16),
            pltpu.VMEM((CHUNKS, ROWS, HID), BF16),
            pltpu.VMEM((CHUNKS, ROWS, HID), BF16),
            pltpu.VMEM((CHUNKS, 2, NX, HALF, WIDE), BF16),
            pltpu.VMEM((CHUNKS, NX, HALF, WIDE), BF16),
            pltpu.VMEM((CHUNKS, NX, HALF, WIDE), BF16),
            pltpu.VMEM((CHUNKS, HALF // 2, WIDE), BF16),
            pltpu.VMEM((CHUNKS, HALF // 2, WIDE), BF16),
            pltpu.VMEM((CHUNKS, HALF, WIDE), BF16),
            pltpu.VMEM((CHUNKS, HALF, WIDE), BF16),
            pltpu.VMEM((CHUNKS, HALF, WIDE), BF16),
            pltpu.VMEM((CHUNKS, HALF, WIDE), BF16),
            pltpu.VMEM((2, WIDE, TOK), F32),
            dma((3,)),
        ]
        + [per_chunk] * 26
        + [per_chunk, per_chunk, dma, dma, dma],
        compiler_params=pltpu.CompilerParams(
            collective_id=0, has_side_effects=True, vmem_limit_bytes=56 * 1024 * 1024
        ),
    )(
        x_stash.T, out_grad.T, by_block(expert_ids), by_block(gates), scales.reshape(blocks, TOK),
        w_gate[0], w_up[0], w_down[0].T,
    )
    return grad_input.T, grad_gate[None], grad_up[None], grad_down.T[None]


def solution(mesh):
    return jax.shard_map(
        on_device,
        mesh=mesh,
        in_specs=(
            P("expert", "dp"),
            P("expert", "dp"),
            P(),
            P(),
            P(),
            P("expert", None, "dp"),
            P("expert", None, "dp"),
            P("expert", "dp", None),
        ),
        out_specs=(
            P("expert", "dp"),
            P("expert", None, "dp"),
            P("expert", None, "dp"),
            P("expert", "dp", None),
        ),
        check_vma=False,
    )
```

time: 122 us -> 105 us (0.86)
  local copies, waits for them, and re-layouts: 17.6 us -> 5.76 us
  other arithmetic: 5.84 us -> 0 us
  Pallas kernels: 96.6 us -> 98.1 us
    another operation x10 -> x0, local copies, waits for them, and re-layouts: 3.99 us -> none  [the longest x3 2.98 us: on_device(): return (grad_input, grad_gate[None], grad_up[None], grad_down[None])]
    concatenate x3 -> x0, other arithmetic: 3.56 us -> none  [the longest x1 1.52 us: on_device(): w_gu = jnp.concatenate([by_owner(w_gate[0]), by_owner(w_up[0])], axis=1)]
    reshape x4 -> x0, local copies, waits for them, and re-layouts: 3.29 us -> none  [the longest x2 2.06 us: relative(): a = a.reshape(TOP, NZ, NY, TOK)]
    unnamed x15 -> x8, local copies, waits for them, and re-layouts: 2.64 us -> 5.76 us
    transpose x2 -> x0, local copies, waits for them, and re-layouts: 2.18 us -> none  [on_device(): gd[:, :, :, shift:shift + FEAT].transpose(2, 0, 1, 3).reshape(HID, d)]
    convert_element_type x5 -> x0, local copies, waits for them, and re-layouts: 1.92 us -> none  [the longest x1 1 us: on_device(): grad_input = lax.dynamic_slice_in_dim(total, c * FEAT, FEAT, 1).astype(BF16)]
    pallas_call x1, Pallas kernels: 96.6 us -> 98.1 us  [on_device(): pl.pallas_call(kernel, out_shape=(jax.ShapeDtypeStruct((FEAT, TOK), BF16)...]
    dynamic_slice x4 -> x0, local copies, waits for them, and re-layouts: 1.47 us -> none  [the longest x1 0.77 us: on_device(): scale = lax.dynamic_slice_in_dim(scales, ex * TOK, TOK, 0)]
where the time goes in v2:
time: 105 us
  Pallas kernels  98.1 us (93%)
  local copies, waits for them, and re-layouts  5.76 us (5%)
    pallas_call x1, Pallas kernels, on_device(): pl.pallas_call(kernel, out_shape=(jax.ShapeDtypeStruct((FEAT, TOK), BF16)...  98.1 us
    unnamed x8, local copies, waits for them, and re-layouts  5.76 us

profile of v2, /device:TPU:1, one launch (start us, length us, event | category | flops | bytes accessed | tf_op | source)
XLA Modules:
  0.0 104.6 jit_solution(14693142280430748963)
XLA Ops:
  0.6 98.1 %shard_map.111 = (bf16[180,128]{1,0:T(8,128)(2,1)}, bf16[1440,256]{1,0:T(8,128)(2,1)}, bf16[1440,256]{1,0:T(8,128)(2,1)}, bf16[1440,256]{1,0:T(8,128)(2,1)}) custom-call(bf16[180,128]{1,0:T(8,128)(2,1)} %bitcast.28, bf16[180,128]{1,0:T(8,128)(2,1)} %bitcast.29, s32[64,4,128]{2,1,0:T(4,128)} %bitcast.26, f32[64,4,128]{2,1,0:T(4,128)} %bitcast.27, ...), custom_call_target="tpu_custom_call" | custom-call | tf_op jit(solution)/shard_map/pallas_call | solution.py:428
  98.8 1.4 %copy.16 = bf16[128,180]{0,1:T(8,128)(2,1)} copy(bf16[128,180]{0,1:T(8,128)(2,1)} %bitcast.30) | data formatting | bytes 92160
  100.2 0.0 copy-start.1
  100.2 2.1 %copy.17 = bf16[1,1440,256]{2,1,0:T(8,128)(2,1)} copy(bf16[1,1440,256]{2,1,0:T(8,128)(2,1)} %bitcast.25) | data formatting | bytes 1474560
  102.3 0.0 copy-done.1
  102.3 0.0 copy-start
  102.3 0.9 copy.18
  103.2 0.5 copy-done
  103.7 0.9 copy.19
Async XLA Ops:
  100.2 2.1 %copy-start.1 = (bf16[1440,256]{1,0:T(8,128)(2,1)S(1)}, bf16[1440,256]{1,0:T(8,128)(2,1)}, u32[]{:S(2)}) copy-start(bf16[1440,256]{1,0:T(8,128)(2,1)} %get-tuple-element.10) | copy-start | bytes 2211844
  102.3 1.4 %copy-start = (bf16[1440,256]{1,0:T(8,128)(2,1)S(1)}, bf16[1440,256]{1,0:T(8,128)(2,1)}, u32[]{:S(2)}) copy-start(bf16[1440,256]{1,0:T(8,128)(2,1)} %get-tuple-element.11) | copy-start | bytes 2211844

commit v3 on v2

--- a/solution.py
+++ b/solution.py
@@ -15,7 +15,8 @@
 HID = 256
 HALF = NY * SLOTS
 ROWS = 2 * HALF
-LAG = 7
+LAG = 6
+PARTS = 2
 F32 = jnp.float32
 BF16 = jnp.bfloat16
 
@@ -33,15 +34,15 @@
 
 
 def far(i):
-    return (i >> 1) + (CHUNKS // 2) * (i & 1)
+    return i
 
 
 def kernel(
     x_in, dy_in, ids, gates, scales, wg_hbm, wu_hbm, wd_hbm,
     gi_out, gg_out, gu_out, gd_out,
     wg, wu, wdt, w_in, sel, gate, xs_buf, dy_buf,
-    zp, zm, yb, g, dgbuf, dubuf, abuf, pb, sb, q, rl, rr, fl, fr, back, ret, fin,
-    w_sem, zp_s, zp_r, zm_s, zm_r, y_s, y_r, xr_s, xr_r, xl_s, xl_r, xfr_s, xfr_r, xfl_s, xfl_r,
+    zp, zm, yb, g, dgbuf, dubuf, abuf, pb, sb, q, rl, rr, fl, fr, back, ret, fin, grads,
+    w_sem, out_sem, zp_s, zp_r, zm_s, zm_r, y_s, y_r, xr_s, xr_r, xl_s, xl_r, xfr_s, xfr_r, xfl_s, xfl_r,
     sib_s, sib_r, ps_s, ps_r, ar_s, ar_r, al_s, al_r, br_s, br_r, bl_s, bl_r,
     ret_s, ret0_s, ret_r, fin_s, fin_r,
 ):
@@ -74,9 +75,6 @@
     def take(ref, sem):
         pltpu.make_async_copy(ref, ref, sem).wait()
 
-    jump = CHUNKS // 2
-    express_right = dev(x, c, y, (z + jump) % NZ)
-    express_left = dev(x, c, y, (z + NZ - jump - 1) % NZ)
     weights = [
         pltpu.make_async_copy(src, dst, w_sem.at[n])
         for n, (src, dst) in enumerate(((wg_hbm, wg), (wu_hbm, wu), (wd_hbm, wdt)))
@@ -85,10 +83,7 @@
         copy.start()
 
     barrier = pltpu.get_barrier_semaphore()
-    for to in (
-        zright, zleft, xright, xleft, sibling,
-        dev(x, c, y, (z + NZ - jump) % NZ), dev(x, c, y, (z + jump + 1) % NZ),
-    ):
+    for to in (zright, zleft, xright, xleft, sibling):
         pl.semaphore_signal(barrier, inc=1, device_id=to, device_id_type=pl.DeviceIdType.MESH)
     for d in range(1, NY):
         pl.semaphore_signal(
@@ -96,40 +91,33 @@
             device_id_type=pl.DeviceIdType.MESH,
         )
 
-    @pl.loop(0, CHUNKS)
-    def _(i):
-        for d in range(NY):
-            def send_signal():
-                pl.semaphore_signal(
-                    barrier, inc=1, device_id=dev(x, c, (y + d) % NY, ret_from(i)),
-                    device_id_type=pl.DeviceIdType.MESH,
-                )
-
-            if d == 0:
-                pl.when((c == 1) | (i > 0))(send_signal)
-            else:
-                send_signal()
-
     xs_own = (x_in[...].astype(F32) * scales[pl.ds(ex, 1), :]).astype(BF16).astype(F32)
     own = [xs_own, dy_in[...].astype(F32), jnp.zeros((WIDE - 2 * FEAT, TOK), F32)]
     zp[0] = jnp.concatenate(own, axis=0).astype(BF16).T
 
-    pl.semaphore_wait(barrier, 10 + CHUNKS * NY - jnp.where(c == 0, 1, 0))
-
-    def z_right(i):
-        return rc(zp.at[i], zp.at[i + 2], zp_s.at[i], zp_r.at[i + 2], zright)
-
-    def z_left(i):
-        return rc(zm.at[i], zm.at[i + 2], zm_s.at[i], zm_r.at[i + 2], zleft)
-
-    first = (
-        rc(zp.at[0], zp.at[2], zp_s.at[0], zp_r.at[2], zright),
-        rc(zp.at[0], zm.at[0], zm_s.at[CHUNKS - 1], zm_r.at[0], zleft),
-        rc(zp.at[0], zp.at[1], zp_s.at[CHUNKS - 1], zp_r.at[1], express_right),
-        rc(zp.at[0], zm.at[1], zm_s.at[CHUNKS - 2], zm_r.at[1], express_left),
-    )
-    for copy in first:
-        copy.start()
+    pl.semaphore_wait(barrier, 5 + NY - 1)
+
+    def part(n):
+        return pl.ds(n * (TOK // PARTS), TOK // PARTS)
+
+    def z_right(i, n):
+        return rc(
+            zp.at[i, part(n)], zp.at[i + 1, part(n)], zp_s.at[i, n], zp_r.at[i + 1, n], zright
+        )
+
+    def z_left(i, n):
+        return rc(
+            zm.at[i, part(n)], zm.at[i + 1, part(n)], zm_s.at[i, n], zm_r.at[i + 1, n], zleft
+        )
+
+    def z_first(n):
+        return rc(
+            zp.at[0, part(n)], zm.at[0, part(n)], zm_s.at[CHUNKS - 1, n], zm_r.at[0, n], zleft
+        )
+
+    for n in range(PARTS):
+        z_first(n).start()
+        z_right(0, n).start()
 
     def origins(i):
         return (z + NZ - far(i)) % NZ, (z + far(i) + 1) % NZ
@@ -175,19 +163,20 @@
         )
 
     def stage_z(i):
-        take(zm.at[i], zm_r.at[i])
-
-        @pl.when(i < CHUNKS - 2)
-        def _():
-            z_left(i).start()
-
-        @pl.when(i > 0)
-        def _():
-            take(zp.at[i], zp_r.at[i])
-
-            @pl.when(i < CHUNKS - 2)
+        for n in range(PARTS):
+            take(zm.at[i, part(n)], zm_r.at[i, n])
+
+            @pl.when(i < CHUNKS - 1)
             def _():
-                z_right(i).start()
+                z_left(i, n).start()
+
+            @pl.when(i > 0)
+            def _():
+                take(zp.at[i, part(n)], zp_r.at[i, n])
+
+                @pl.when(i < CHUNKS - 1)
+                def _():
+                    z_right(i, n).start()
 
         for h, src in ((0, zp), (1, zm)):
             yb[i, h] = jnp.dot(
@@ -318,7 +307,7 @@
 
     stages = (
         (stage_z, 0), (stage_x1, 1), (stage_x2, 2), (stage_x3, 3),
-        (stage_c, 4), (stage_r1, 5), (stage_r2, 6), (stage_r3, 7),
+        (stage_r1, 4), (stage_r2, 5), (stage_r3, 6), (stage_c, 3),
     )
 
     def prepare_in():
@@ -337,17 +326,20 @@
     def flat(ref):
         return ref[...].reshape(CHUNKS * ROWS, ref.shape[-1])
 
-    def over_slots(a, b, out):
-        out[...] = lax.dot_general(
+    def grad_copy(n):
+        return pltpu.make_async_copy(grads.at[n], (gg_out, gu_out, gd_out)[n], out_sem.at[n])
+
+    def over_slots(a, b, n):
+        grads[n] = lax.dot_general(
             flat(a), flat(b), over_rows, preferred_element_type=F32
         ).astype(BF16)
+        grad_copy(n).start()
 
     extra = {
         0: lambda: pl.loop(0, CHUNKS)(prepare_gate),
         1: prepare_in,
-        CHUNKS + LAG - 3: lambda: over_slots(xs_buf, dgbuf, gg_out),
-        CHUNKS + LAG - 2: lambda: over_slots(xs_buf, dubuf, gu_out),
-        CHUNKS + LAG - 1: lambda: over_slots(dy_buf, abuf, gd_out),
+        CHUNKS + LAG - 2: lambda: over_slots(xs_buf, dgbuf, 0),
+        CHUNKS + LAG - 1: lambda: over_slots(xs_buf, dubuf, 1),
     }
 
     @pl.loop(0, CHUNKS + LAG)
@@ -359,8 +351,11 @@
             def _():
                 stage(i)
 
-        for at, work in extra.items():
-            pl.when(step == at)(work)
+            if stage is stage_c:
+                for at, work in extra.items():
+                    pl.when(step == at)(work)
+
+    over_slots(dy_buf, abuf, 2)
 
     order = lax.broadcasted_iota(jnp.int32, (CHUNKS * NY, TOK), 0)
     step_of, y_of = order >> 2, order & (NY - 1)
@@ -381,13 +376,11 @@
 
     @pl.loop(0, CHUNKS)
     def _(i):
-        @pl.when(i < CHUNKS - 2)
+        @pl.when(i < CHUNKS - 1)
         def _():
-            z_left(i).wait_send()
-
-            @pl.when(i > 0)
-            def _():
-                z_right(i).wait_send()
+            for n in range(PARTS):
+                z_left(i, n).wait_send()
+                z_right(i, n).wait_send()
 
         take(yb.at[i, :, pl.ds(0, (NY - 1) * SLOTS), :], y_s.at[i])
         x_right(i).wait_send()
@@ -406,11 +399,18 @@
         def _():
             ret_send(i, 0, ret0_s.at[i]).wait_send()
 
-    for copy in first:
-        copy.wait_send()
+    for n in range(PARTS):
+        z_first(n).wait_send()
+    for n in range(3):
+        grad_copy(n).wait()
     last.wait()
     total = fin[0] + fin[1]
     gi_out[...] = jnp.where(c == 0, total[:FEAT], total[FEAT : 2 * FEAT]).astype(BF16)
+
+
+def hand_over(*refs):
+    for n in range(4):
+        refs[n + 4][...] = refs[n][...]
 
 
 def on_device(x_stash, out_grad, expert_ids, gates, scales, w_gate, w_up, w_down):
@@ -425,7 +425,7 @@
     block = (CHUNKS, 2, HALF, WIDE)
     dma = pltpu.SemaphoreType.DMA
     per_chunk = dma((CHUNKS,))
-    grad_input, grad_gate, grad_up, grad_down = pl.pallas_call(
+    results = pl.pallas_call(
         kernel,
         out_shape=(
             jax.ShapeDtypeStruct((FEAT, TOK), BF16),
@@ -434,7 +434,7 @@
             jax.ShapeDtypeStruct((d, HID), BF16),
         ),
         in_specs=[vmem] * 5 + [hbm] * 3,
-        out_specs=(vmem,) * 4,
+        out_specs=(vmem, hbm, hbm, hbm),
         scratch_shapes=[
             pltpu.VMEM((d, HID), BF16),
             pltpu.VMEM((d, HID), BF16),
@@ -461,9 +461,12 @@
             pltpu.VMEM((CHUNKS, HALF, WIDE), BF16),
             pltpu.VMEM((CHUNKS, HALF, WIDE), BF16),
             pltpu.VMEM((2, WIDE, TOK), F32),
+            pltpu.VMEM((3, d, HID), BF16),
+            dma((3,)),
             dma((3,)),
         ]
-        + [per_chunk] * 26
+        + [dma((CHUNKS, PARTS))] * 4
+        + [per_chunk] * 22
         + [per_chunk, per_chunk, dma, dma, dma],
         compiler_params=pltpu.CompilerParams(
             collective_id=0, has_side_effects=True, vmem_limit_bytes=56 * 1024 * 1024
@@ -472,6 +475,12 @@
         x_stash.T, out_grad.T, by_block(expert_ids), by_block(gates), scales.reshape(blocks, TOK),
         w_gate[0], w_up[0], w_down[0].T,
     )
+    grad_input, grad_gate, grad_up, grad_down = pl.pallas_call(
+        hand_over,
+        out_shape=tuple(jax.ShapeDtypeStruct(r.shape, r.dtype) for r in results),
+        in_specs=[vmem] * 4,
+        out_specs=(vmem,) * 4,
+    )(*results)
     return grad_input.T, grad_gate[None], grad_up[None], grad_down.T[None]
 
 

time: 105 us -> 93.6 us (0.89)
  local copies, waits for them, and re-layouts: 5.76 us -> 0 us
  Pallas kernels: 98.1 us -> 92.8 us
    pallas_call x1, Pallas kernels: 98.1 us -> 89.8 us  [on_device(): pl.pallas_call(kernel, out_shape=(jax.ShapeDtypeStruct((FEAT, TOK), BF16)...]
    unnamed x8 -> x0, local copies, waits for them, and re-layouts: 5.76 us -> none
    pallas_call x0 -> x1, Pallas kernels: none -> 2.99 us  [on_device(): pl.pallas_call(hand_over, out_shape=tuple((jax.ShapeDtypeStruct(r.shape,...]
where the time goes in v3:
time: 93.6 us; the launch traced here: 93.4 us
  Pallas kernels  92.8 us (99%)
    pallas_call x1, Pallas kernels, on_device(): pl.pallas_call(kernel, out_shape=(jax.ShapeDtypeStruct((FEAT, TOK), BF16)...  89.8 us
    pallas_call x1, Pallas kernels, on_device(): pl.pallas_call(hand_over, out_shape=tuple((jax.ShapeDtypeStruct(r.shape,...  2.99 us

profile of v3, /device:TPU:1, one launch (start us, length us, event | category | flops | bytes accessed | tf_op | source)
XLA Modules:
  0.0 93.4 jit_solution(6298335189196947099)
XLA Ops:
  0.6 89.8 %shard_map.111 = (bf16[180,128]{1,0:T(8,128)(2,1)}, bf16[1440,256]{1,0:T(8,128)(2,1)}, bf16[1440,256]{1,0:T(8,128)(2,1)}, bf16[1440,256]{1,0:T(8,128)(2,1)}) custom-call(bf16[180,128]{1,0:T(8,128)(2,1)} %bitcast.25, bf16[180,128]{1,0:T(8,128)(2,1)} %bitcast.26, s32[64,4,128]{2,1,0:T(4,128)} %bitcast.23, f32[64,4,128]{2,1,0:T(4,128)} %bitcast.24, ...), custom_call_target="tpu_custom_call" | custom-call | tf_op jit(solution)/shard_map/pallas_call | solution.py:428
  90.4 3.0 %shard_map.112 = (bf16[180,128]{1,0:T(8,128)(2,1)}, bf16[1440,256]{1,0:T(8,128)(2,1)}, bf16[1440,256]{1,0:T(8,128)(2,1)}, bf16[1440,256]{1,0:T(8,128)(2,1)}) custom-call(bf16[180,128]{1,0:T(8,128)(2,1)} %get-tuple-element.12.refs_0_, bf16[1440,256]{1,0:T(8,128)(2,1)} %get-tuple-element.13.refs_1_, bf16[1440,256]{1,0:T(8,128)(2,1)} %get-tuple-element.14.refs_2_, ...), custom_call_target="tpu_custom_call" | custom-call | tf_op jit(solution)/shard_map/pallas_call | solution.py:478

commit v4 on v3

--- a/solution.py
+++ b/solution.py
@@ -1,3 +1,5 @@
+import functools
+
 import jax
 import jax.numpy as jnp
 from jax import lax
@@ -15,8 +17,10 @@
 HID = 256
 HALF = NY * SLOTS
 ROWS = 2 * HALF
-LAG = 6
 PARTS = 2
+DIRECT_X = 8
+LATE = 1
+DIRECT_R = 5
 F32 = jnp.float32
 BF16 = jnp.bfloat16
 
@@ -34,7 +38,7 @@
 
 
 def far(i):
-    return i
+    return jnp.where(i == CHUNKS - 1, LATE, i + (i >= LATE).astype(jnp.int32))
 
 
 def kernel(
@@ -83,7 +87,8 @@
         copy.start()
 
     barrier = pltpu.get_barrier_semaphore()
-    for to in (zright, zleft, xright, xleft, sibling):
+    xfar = dev(xo, c, y, z)
+    for to in (zright, zleft, xright, xleft, xfar, sibling):
         pl.semaphore_signal(barrier, inc=1, device_id=to, device_id_type=pl.DeviceIdType.MESH)
     for d in range(1, NY):
         pl.semaphore_signal(
@@ -95,7 +100,7 @@
     own = [xs_own, dy_in[...].astype(F32), jnp.zeros((WIDE - 2 * FEAT, TOK), F32)]
     zp[0] = jnp.concatenate(own, axis=0).astype(BF16).T
 
-    pl.semaphore_wait(barrier, 5 + NY - 1)
+    pl.semaphore_wait(barrier, 6 + NY - 1)
 
     def part(n):
         return pl.ds(n * (TOK // PARTS), TOK // PARTS)
@@ -162,7 +167,7 @@
             y_s.at[i], y_r.at[i], dev(x, c, to, z),
         )
 
-    def stage_z(i):
+    def stage_ring(i):
         for n in range(PARTS):
             take(zm.at[i, part(n)], zm_r.at[i, n])
 
@@ -178,9 +183,10 @@
                 def _():
                     z_right(i, n).start()
 
+    def stage_z(i):
         for h, src in ((0, zp), (1, zm)):
             yb[i, h] = jnp.dot(
-                sel[i, pl.ds(h * HALF, HALF)], src[i], preferred_element_type=F32
+                sel[i, pl.ds(h * HALF, HALF)], src[far(i)], preferred_element_type=F32
             ).astype(BF16)
         for d in range(1, NY):
             y_send(i, d).start()
@@ -191,11 +197,11 @@
     def sib_send(i, x_):
         return rc(g.at[c, x_, i], g.at[c, x_, i], sib_s.at[i], sib_r.at[i], sibling)
 
-    def x_right(i):
-        return rc(g.at[c, x, i], g.at[c, x, i], xr_s.at[i], xr_r.at[i], xright)
-
-    def x_left(i):
-        return rc(g.at[c, x, i], g.at[c, x, i], xl_s.at[i], xl_r.at[i], xleft)
+    def x_right(i, h):
+        return rc(g.at[c, x, i, h], g.at[c, x, i, h], xr_s.at[i, h], xr_r.at[i, h], xright)
+
+    def x_left(i, h):
+        return rc(g.at[c, x, i, h], g.at[c, x, i, h], xl_s.at[i, h], xl_r.at[i, h], xleft)
 
     def x_far_right(i):
         return rc(g.at[c, xl, i, 0], g.at[c, xl, i, 0], xfr_s.at[i], xfr_r.at[i], xright)
@@ -203,21 +209,39 @@
     def x_far_left(i):
         return rc(g.at[c, xr, i, 1], g.at[c, xr, i, 1], xfl_s.at[i], xfl_r.at[i], xleft)
 
+    def x_direct(i, h):
+        s, r = ((xfr_s, xfr_r), (xfl_s, xfl_r))[h]
+        return rc(g.at[c, x, i, h], g.at[c, x, i, h], s.at[i], r.at[i], xfar)
+
     def stage_x1(i):
         take(g.at[c, x, i], y_r.at[i])
-        x_right(i).start()
-        x_left(i).start()
+        x_right(i, 0).start()
+        x_left(i, 1).start()
+        x_right(i, 1).start()
+        x_left(i, 0).start()
+
+        @pl.when(i >= DIRECT_X)
+        def _():
+            x_direct(i, 0).start()
+            x_direct(i, 1).start()
+
         sib_send(i, x).start()
 
     def stage_x2(i):
-        take(g.at[c, xl, i], xr_r.at[i])
-        x_far_right(i).start()
-        take(g.at[c, xr, i], xl_r.at[i])
-        x_far_left(i).start()
+        take(g.at[c, xl, i, 0], xr_r.at[i, 0])
+        take(g.at[c, xr, i, 1], xl_r.at[i, 1])
+
+        @pl.when(i < DIRECT_X)
+        def _():
+            x_far_right(i).start()
+            x_far_left(i).start()
+
+    def stage_x3(i):
+        pl.when(i >= DIRECT_X)(lambda: stage_x2(i))
+        take(g.at[c, xl, i, 1], xr_r.at[i, 1])
         sib_send(i, xl).start()
+        take(g.at[c, xr, i, 0], xl_r.at[i, 0])
         sib_send(i, xr).start()
-
-    def stage_x3(i):
         take(g.at[c, xo, i, 0], xfr_r.at[i])
         take(g.at[c, xo, i, 1], xfl_r.at[i])
         sib_send(i, xo).start()
@@ -253,32 +277,47 @@
 
     quarter = HALF // 2
 
-    def a_right(i):
-        return rc(q.at[i, xo, pl.ds(0, quarter)], rl.at[i], ar_s.at[i], ar_r.at[i], xright)
-
-    def a_left(i):
-        return rc(q.at[i, xo, pl.ds(quarter, quarter)], rr.at[i], al_s.at[i], al_r.at[i], xleft)
-
-    def b_right(i):
-        return rc(q.at[i, xr], fl.at[i], br_s.at[i], br_r.at[i], xright)
-
-    def b_left(i):
-        return rc(q.at[i, xl], fr.at[i], bl_s.at[i], bl_r.at[i], xleft)
+    def side(h):
+        return pl.ds(h * quarter, quarter)
+
+    def a_right(i, to):
+        return rc(q.at[i, xo, side(0)], rl.at[i], ar_s.at[i], ar_r.at[i], to)
+
+    def a_left(i, to):
+        return rc(q.at[i, xo, side(1)], rr.at[i], al_s.at[i], al_r.at[i], to)
+
+    def b_right(i, h):
+        return rc(q.at[i, xr, side(h)], fl.at[i, side(h)], br_s.at[i, h], br_r.at[i, h], xright)
+
+    def b_left(i, h):
+        return rc(q.at[i, xl, side(h)], fr.at[i, side(h)], bl_s.at[i, h], bl_r.at[i, h], xleft)
 
     def stage_r1(i):
         take(sb.at[i], ps_r.at[i])
         q[i] = (pb[i, c].astype(F32) + sb[i].astype(F32)).astype(BF16)
-        a_right(i).start()
-        a_left(i).start()
+
+        @pl.when(i < DIRECT_R)
+        def _():
+            a_right(i, xright).start()
+            a_left(i, xleft).start()
+
+        @pl.when(i >= DIRECT_R)
+        def _():
+            a_right(i, xfar).start()
+            a_left(i, xfar).start()
+            b_right(i, 0).start()
+            b_left(i, 1).start()
+
+        b_right(i, 1).start()
+        b_left(i, 0).start()
 
     def stage_r2(i):
         take(rl.at[i], ar_r.at[i])
-        lo, hi = pl.ds(0, quarter), pl.ds(quarter, quarter)
-        q[i, xr, lo] = (q[i, xr, lo].astype(F32) + rl[i].astype(F32)).astype(BF16)
-        b_right(i).start()
+        q[i, xr, side(0)] = (q[i, xr, side(0)].astype(F32) + rl[i].astype(F32)).astype(BF16)
+        b_right(i, 0).start()
         take(rr.at[i], al_r.at[i])
-        q[i, xl, hi] = (q[i, xl, hi].astype(F32) + rr[i].astype(F32)).astype(BF16)
-        b_left(i).start()
+        q[i, xl, side(1)] = (q[i, xl, side(1)].astype(F32) + rr[i].astype(F32)).astype(BF16)
+        b_left(i, 1).start()
 
     def ret_send(i, d, sem):
         to = (y + d) % NY
@@ -288,9 +327,22 @@
         )
 
     def stage_r3(i):
-        take(fl.at[i], br_r.at[i])
-        take(fr.at[i], bl_r.at[i])
-        back[i] = (q[i, x].astype(F32) + fl[i].astype(F32) + fr[i].astype(F32)).astype(BF16)
+        for h in range(2):
+            take(fl.at[i, side(h)], br_r.at[i, h])
+            take(fr.at[i, side(h)], bl_r.at[i, h])
+        total = q[i, x].astype(F32) + fl[i].astype(F32) + fr[i].astype(F32)
+
+        @pl.when(i < DIRECT_R)
+        def _():
+            back[i] = total.astype(BF16)
+
+        @pl.when(i >= DIRECT_R)
+        def _():
+            take(rl.at[i], ar_r.at[i])
+            take(rr.at[i], al_r.at[i])
+            across = jnp.concatenate([rl[i].astype(F32), rr[i].astype(F32)], axis=0)
+            back[i] = (total + across).astype(BF16)
+
         for d in range(1, NY):
             ret_send(i, d, ret_s.at[i]).start()
         local = (c == 0) & (i == 0)
@@ -305,10 +357,20 @@
         def _():
             ret_send(i, 0, ret0_s.at[i]).start()
 
+    def at_step(lag, *direct):
+        return [i + lag - sum(i >= first for first in direct) for i in range(CHUNKS)]
+
     stages = (
-        (stage_z, 0), (stage_x1, 1), (stage_x2, 2), (stage_x3, 3),
-        (stage_r1, 4), (stage_r2, 5), (stage_r3, 6), (stage_c, 3),
+        (stage_z, at_step(0)),
+        (stage_x1, at_step(1)),
+        (stage_x2, at_step(2)[:DIRECT_X]),
+        (stage_x3, at_step(3, DIRECT_X)),
+        (stage_r1, at_step(4, DIRECT_X)),
+        (stage_r2, at_step(5, DIRECT_X)[:DIRECT_R]),
+        (stage_r3, at_step(6, DIRECT_X, DIRECT_R)),
+        (stage_c, at_step(3, DIRECT_X)),
     )
+    steps = stages[-2][1][-1] + 1
 
     def prepare_in():
         for copy in weights:
@@ -338,20 +400,25 @@
     extra = {
         0: lambda: pl.loop(0, CHUNKS)(prepare_gate),
         1: prepare_in,
-        CHUNKS + LAG - 2: lambda: over_slots(xs_buf, dgbuf, 0),
-        CHUNKS + LAG - 1: lambda: over_slots(xs_buf, dubuf, 1),
+        steps - 2: lambda: over_slots(xs_buf, dgbuf, 0),
+        steps - 1: lambda: over_slots(xs_buf, dubuf, 1),
     }
 
-    @pl.loop(0, CHUNKS + LAG)
+    @pl.loop(0, steps)
     def _(step):
-        for stage, lag in stages:
-            i = step - lag
-
-            @pl.when((i >= 0) & (i < CHUNKS))
-            def _():
-                stage(i)
+        ring = step + (step >= LATE).astype(jnp.int32)
+        pl.when(ring < CHUNKS)(lambda: stage_ring(ring))
+        for stage, when in stages:
+            if when == list(range(when[0], when[0] + len(when))):
+                i = step - when[0]
+                pl.when((i >= 0) & (i < len(when)))(functools.partial(stage, i))
+            else:
+                low = sum((step > t).astype(jnp.int32) for t in when)
+                high = sum((step >= t).astype(jnp.int32) for t in when)
+                pl.loop(low, high)(stage)
 
             if stage is stage_c:
+                pl.when(step == LATE - 1)(lambda: stage_ring(step + 1))
                 for at, work in extra.items():
                     pl.when(step == at)(work)
 
@@ -383,16 +450,17 @@
                 z_right(i, n).wait_send()
 
         take(yb.at[i, :, pl.ds(0, (NY - 1) * SLOTS), :], y_s.at[i])
-        x_right(i).wait_send()
-        x_left(i).wait_send()
+        for h in range(2):
+            x_right(i, h).wait_send()
+            x_left(i, h).wait_send()
+            b_right(i, h).wait_send()
+            b_left(i, h).wait_send()
         x_far_right(i).wait_send()
         x_far_left(i).wait_send()
         take(g.at[c, :, i], sib_s.at[i])
         p_send(i).wait_send()
-        a_right(i).wait_send()
-        a_left(i).wait_send()
-        b_right(i).wait_send()
-        b_left(i).wait_send()
+        a_right(i, xright).wait_send()
+        a_left(i, xleft).wait_send()
         take(back.at[i, pl.ds(0, (NY - 1) * SLOTS), :], ret_s.at[i])
 
         @pl.when((c == 1) | (i > 0))
@@ -409,8 +477,16 @@
 
 
 def hand_over(*refs):
+    ins, outs, held, sem = refs[:4], refs[4:8], refs[8:12], refs[12]
+    load = [pltpu.make_async_copy(ins[n], held[n], sem.at[0, n]) for n in range(4)]
+    store = [pltpu.make_async_copy(held[n], outs[n], sem.at[1, n]) for n in range(4)]
+    for copy in load:
+        copy.start()
     for n in range(4):
-        refs[n + 4][...] = refs[n][...]
+        load[n].wait()
+        store[n].start()
+    for copy in store:
+        copy.wait()
 
 
 def on_device(x_stash, out_grad, expert_ids, gates, scales, w_gate, w_up, w_down):
@@ -466,7 +542,10 @@
             dma((3,)),
         ]
         + [dma((CHUNKS, PARTS))] * 4
-        + [per_chunk] * 22
+        + [per_chunk] * 2
+        + [dma((CHUNKS, 2))] * 4
+        + [per_chunk] * 12
+        + [dma((CHUNKS, 2))] * 4
         + [per_chunk, per_chunk, dma, dma, dma],
         compiler_params=pltpu.CompilerParams(
             collective_id=0, has_side_effects=True, vmem_limit_bytes=56 * 1024 * 1024
@@ -478,8 +557,10 @@
     grad_input, grad_gate, grad_up, grad_down = pl.pallas_call(
         hand_over,
         out_shape=tuple(jax.ShapeDtypeStruct(r.shape, r.dtype) for r in results),
-        in_specs=[vmem] * 4,
-        out_specs=(vmem,) * 4,
+        in_specs=[hbm] * 4,
+        out_specs=(hbm,) * 4,
+        scratch_shapes=[pltpu.VMEM(r.shape, r.dtype) for r in results] + [dma((2, 4))],
+        compiler_params=pltpu.CompilerParams(vmem_limit_bytes=60 * 1024 * 1024),
     )(*results)
     return grad_input.T, grad_gate[None], grad_up[None], grad_down.T[None]
 

time: 93.6 us -> 91.8 us (0.981)
  Pallas kernels: 92.8 us -> 91 us
    pallas_call x1, Pallas kernels: 89.8 us -> 88.4 us  [on_device(): pl.pallas_call(kernel, out_shape=(jax.ShapeDtypeStruct((FEAT, TOK), BF16)...]
where the time goes in v4:
time: 91.8 us; the launch traced here: 91.7 us
  Pallas kernels  91 us (99%)
    pallas_call x1, Pallas kernels, on_device(): pl.pallas_call(kernel, out_shape=(jax.ShapeDtypeStruct((FEAT, TOK), BF16)...  88.4 us
    pallas_call x1, Pallas kernels, on_device(): pl.pallas_call(hand_over, out_shape=tuple((jax.ShapeDtypeStruct(r.shape,...  2.56 us

profile of v4, /device:TPU:1, one launch (start us, length us, event | category | flops | bytes accessed | tf_op | source)
XLA Modules:
  0.0 91.7 jit_solution(6976770154784661190)
XLA Ops:
  0.6 88.4 %shard_map.111 = (bf16[180,128]{1,0:T(8,128)(2,1)}, bf16[1440,256]{1,0:T(8,128)(2,1)}, bf16[1440,256]{1,0:T(8,128)(2,1)}, bf16[1440,256]{1,0:T(8,128)(2,1)}) custom-call(bf16[180,128]{1,0:T(8,128)(2,1)} %bitcast.25, bf16[180,128]{1,0:T(8,128)(2,1)} %bitcast.26, s32[64,4,128]{2,1,0:T(4,128)} %bitcast.23, f32[64,4,128]{2,1,0:T(4,128)} %bitcast.24, ...), custom_call_target="tpu_custom_call" | custom-call | tf_op jit(solution)/shard_map/pallas_call | solution.py:504
  89.1 2.6 %shard_map.112 = (bf16[180,128]{1,0:T(8,128)(2,1)}, bf16[1440,256]{1,0:T(8,128)(2,1)}, bf16[1440,256]{1,0:T(8,128)(2,1)}, bf16[1440,256]{1,0:T(8,128)(2,1)}) custom-call(bf16[180,128]{1,0:T(8,128)(2,1)} %get-tuple-element.12.refs_0_, bf16[1440,256]{1,0:T(8,128)(2,1)} %get-tuple-element.13.refs_1_, bf16[1440,256]{1,0:T(8,128)(2,1)} %get-tuple-element.14.refs_2_, ...), custom_call_target="tpu_custom_call" | custom-call | tf_op jit(solution)/shard_map/pallas_call | solution.py:557

commit v5 on v4

--- a/solution.py
+++ b/solution.py
@@ -42,9 +42,9 @@
 
 
 def kernel(
-    x_in, dy_in, ids, gates, scales, wg_hbm, wu_hbm, wd_hbm,
+    x_in, dy_in, scales, ids_hbm, gates_hbm, wg_hbm, wu_hbm, wd_hbm,
     gi_out, gg_out, gu_out, gd_out,
-    wg, wu, wdt, w_in, sel, gate, xs_buf, dy_buf,
+    ids, gates, wg, wu, wdt, w_in, sel, gate, xs_buf, dy_buf,
     zp, zm, yb, g, dgbuf, dubuf, abuf, pb, sb, q, rl, rr, fl, fr, back, ret, fin, grads,
     w_sem, out_sem, zp_s, zp_r, zm_s, zm_r, y_s, y_r, xr_s, xr_r, xl_s, xl_r, xfr_s, xfr_r, xfl_s, xfl_r,
     sib_s, sib_r, ps_s, ps_r, ar_s, ar_r, al_s, al_r, br_s, br_r, bl_s, bl_r,
@@ -79,11 +79,12 @@
     def take(ref, sem):
         pltpu.make_async_copy(ref, ref, sem).wait()
 
-    weights = [
-        pltpu.make_async_copy(src, dst, w_sem.at[n])
-        for n, (src, dst) in enumerate(((wg_hbm, wg), (wu_hbm, wu), (wd_hbm, wdt)))
-    ]
-    for copy in weights:
+    pairs = (
+        (ids_hbm, ids), (gates_hbm, gates), (wg_hbm, wg), (wu_hbm, wu), (wd_hbm, wdt),
+    )
+    tables = [pltpu.make_async_copy(src, dst, w_sem.at[n]) for n, (src, dst) in enumerate(pairs)]
+    weights = tables[2:]
+    for copy in tables:
         copy.start()
 
     barrier = pltpu.get_barrier_semaphore()
@@ -155,6 +156,8 @@
         w = jnp.broadcast_to(w[:, None, :], (2 * NY, SLOTS, TOK)).reshape(ROWS, TOK)
         gate[i] = jnp.sum(jnp.where(hot, w, F32(0.0)), axis=1, keepdims=True)
 
+    for copy in tables[:2]:
+        copy.wait()
     pl.loop(0, CHUNKS)(prepare_sel)
 
     def slot_rows(which):
@@ -509,9 +512,11 @@
             jax.ShapeDtypeStruct((d, HID), BF16),
             jax.ShapeDtypeStruct((d, HID), BF16),
         ),
-        in_specs=[vmem] * 5 + [hbm] * 3,
+        in_specs=[vmem] * 3 + [hbm] * 5,
         out_specs=(vmem, hbm, hbm, hbm),
         scratch_shapes=[
+            pltpu.VMEM((blocks, TOP, TOK), jnp.int32),
+            pltpu.VMEM((blocks, TOP, TOK), F32),
             pltpu.VMEM((d, HID), BF16),
             pltpu.VMEM((d, HID), BF16),
             pltpu.VMEM((d, HID), BF16),
@@ -538,7 +543,7 @@
             pltpu.VMEM((CHUNKS, HALF, WIDE), BF16),
             pltpu.VMEM((2, WIDE, TOK), F32),
             pltpu.VMEM((3, d, HID), BF16),
-            dma((3,)),
+            dma((5,)),
             dma((3,)),
         ]
         + [dma((CHUNKS, PARTS))] * 4
@@ -551,7 +556,7 @@
             collective_id=0, has_side_effects=True, vmem_limit_bytes=56 * 1024 * 1024
         ),
     )(
-        x_stash.T, out_grad.T, by_block(expert_ids), by_block(gates), scales.reshape(blocks, TOK),
+        x_stash.T, out_grad.T, scales.reshape(blocks, TOK), by_block(expert_ids), by_block(gates),
         w_gate[0], w_up[0], w_down[0].T,
     )
     grad_input, grad_gate, grad_up, grad_down = pl.pallas_call(

time: 91.8 us -> 91.7 us (level)
  no operation moved by 1% of the time
where the time goes in v5:
time: 91.7 us; the launch traced here: 91.5 us
  Pallas kernels  90.8 us (99%)
    pallas_call x1, Pallas kernels, on_device(): pl.pallas_call(kernel, out_shape=(jax.ShapeDtypeStruct((FEAT, TOK), BF16)...  88.3 us
    pallas_call x1, Pallas kernels, on_device(): pl.pallas_call(hand_over, out_shape=tuple((jax.ShapeDtypeStruct(r.shape,...  2.56 us

profile of v5, /device:TPU:1, one launch (start us, length us, event | category | flops | bytes accessed | tf_op | source)
XLA Modules:
  0.0 91.5 jit_solution(3833177158222226431)
XLA Ops:
  0.6 88.3 %shard_map.111 = (bf16[180,128]{1,0:T(8,128)(2,1)}, bf16[1440,256]{1,0:T(8,128)(2,1)}, bf16[1440,256]{1,0:T(8,128)(2,1)}, bf16[1440,256]{1,0:T(8,128)(2,1)}) custom-call(bf16[180,128]{1,0:T(8,128)(2,1)} %bitcast.25, bf16[180,128]{1,0:T(8,128)(2,1)} %bitcast.26, f32[64,128]{1,0:T(8,128)} %bitcast.27, s32[64,4,128]{2,1,0:T(4,128)} %bitcast.23, ...), custom_call_target="tpu_custom_call" | custom-call | tf_op jit(solution)/shard_map/pallas_call | solution.py:507
  88.9 2.6 %shard_map.112 = (bf16[180,128]{1,0:T(8,128)(2,1)}, bf16[1440,256]{1,0:T(8,128)(2,1)}, bf16[1440,256]{1,0:T(8,128)(2,1)}, bf16[1440,256]{1,0:T(8,128)(2,1)}) custom-call(bf16[180,128]{1,0:T(8,128)(2,1)} %get-tuple-element.12.refs_0_, bf16[1440,256]{1,0:T(8,128)(2,1)} %get-tuple-element.13.refs_1_, bf16[1440,256]{1,0:T(8,128)(2,1)} %get-tuple-element.14.refs_2_, ...), custom_call_target="tpu_custom_call" | custom-call | tf_op jit(solution)/shard_map/pallas_call | solution.py:562
